TPU v7x, 128 devices: a whole 4x4x4 slice. The times are simulated.
128 devices in a mesh: seq: 8 (over z, core), tp: 16 (over x, y).
Axes of the slice: x: 4, y: 4, z: 4, core: 2. Of those that a mesh axis runs over, the one named last changes fastest.
Arguments:
- hidden: bfloat16 [1024, 4096], P('seq', 'tp'), may hold values from -20 to 20
- text_gain: bfloat16 [4096], P('tp'), may hold values from 0.2 to 4
- text_table: bfloat16 [16000, 4096], P('tp'), may hold values from -0.5 to 0.5
- proj: bfloat16 [8, 4096, 1024], P(None, 'tp'), may hold values from -0.09375 to 0.09375
- audio_table: bfloat16 [8, 2048, 1024], P(None, 'tp'), may hold values from -0.75 to 0.75
- depth_gain: bfloat16 [1024], replicated, may hold values from 0.5 to 1.5
- attn_qkv: bfloat16 [1024, 3, 1024], P(None, None, 'tp'), may hold values from -0.1875 to 0.1875
- attn_out: bfloat16 [1024, 1024], P('tp'), may hold values from -0.1875 to 0.1875
- text_ids: int32 [1024], P('seq'), may hold values from 0 to 15999
- audio_ids: int32 [1024, 8], P('seq'), may hold values from 0 to 2047
Outputs:
- losses: float32 [1024, 9], P('seq')
- grad_hidden: float32 [1024, 4096], P('seq', 'tp')
- grad_text_gain: float32 [4096], P('tp')
- grad_text_table: float32 [4096, 16000], P('seq', 'tp')
- grad_proj: float32 [8, 4096, 1024], P(None, 'tp', 'seq')
- grad_audio_table: float32 [8, 2048, 1024], P(None, 'tp', 'seq')
- grad_depth_gain: float32 [1024], replicated
- grad_attn_qkv: float32 [1024, 3, 1024], P('seq', None, 'tp')
- grad_attn_out: float32 [1024, 1024], P('tp', 'seq')
All inputs are finite; a program needn't handle non-finite values.
Results may differ from a plain program's by a relative error of at most 0.022.
Values may be sent and summed in bfloat16 or wider, within the bound.
A program may use at most 128 MiB of HBM per device.

v0:
```python
import math

import jax
import jax.numpy as jnp
from jax import lax
from jax.sharding import PartitionSpec as P

D = 4096
HEAD = 64


soft_cap = 12.0
epsilon = 1e-05


def capped(values):
    return soft_cap * jnp.tanh(values / soft_cap)


def cap_slope(capped_values):
    ratio = capped_values / soft_cap
    return 1.0 - ratio * ratio


def attend(triple):
    frames = triple.shape[0]
    steps = triple.shape[1]
    width = triple.shape[3]
    heads = width // HEAD
    grid = triple.astype(jnp.float32).reshape(frames, steps, 3, heads, HEAD)
    scores = jnp.einsum("fihc,fjhc->fhij", grid[:, :, 0], grid[:, :, 1]) / math.sqrt(HEAD)
    causal = jnp.arange(steps)[:, None] >= jnp.arange(steps)[None, :]
    raised = jnp.where(causal, jnp.exp(scores), 0.0)
    weights = lax.optimization_barrier(
        (raised / jnp.sum(raised, axis=3, keepdims=True)).astype(jnp.bfloat16)
    )
    mixed = jnp.einsum("fhij,fjhc->fihc", weights.astype(jnp.float32), grid[:, :, 2])
    return mixed.reshape(frames, steps, width).astype(jnp.bfloat16)


def on_device(
    hidden,
    text_gain,
    text_table,
    proj,
    audio_table,
    depth_gain,
    attn_qkv,
    attn_out,
    text_ids,
    audio_ids,
):
    frame_count = hidden.shape[0]
    vocab_text = text_table.shape[0]
    vocab_audio = audio_table.shape[1]
    width = audio_table.shape[2]
    tp_rank = lax.axis_index("tp")
    gain_float = depth_gain.astype(jnp.float32)
    hidden_float = hidden.astype(jnp.float32)
    squares = lax.psum(jnp.sum(hidden_float * hidden_float, axis=1), "tp")
    row_scale = lax.rsqrt(squares[:, None] / D + epsilon)
    normed = (hidden_float * row_scale * text_gain.astype(jnp.float32)).astype(jnp.bfloat16)
    full_normed = lax.all_gather(normed, "tp", axis=1, tiled=True)
    hidden_hat = hidden_float * row_scale
    text_logits = capped(
        jnp.einsum("fd,vd->fv", full_normed, text_table, preferred_element_type=jnp.float32)
    )
    text_hot = text_ids[:, None] == (tp_rank * vocab_text + jnp.arange(vocab_text))[None, :]
    text_sum = jnp.sum(jnp.exp(text_logits - soft_cap), axis=1)
    text_chosen = jnp.sum(jnp.where(text_hot, text_logits, 0.0), axis=1)
    embed_scale = math.sqrt(width) / 4.0
    audio_hot = (
        audio_ids[:, :, None] == (tp_rank * vocab_audio + jnp.arange(vocab_audio))[None, None, :]
    )
    hot_values = audio_hot.astype(jnp.bfloat16)
    looked = (
        jnp.einsum("fkv,kve->fke", hot_values, audio_table, preferred_element_type=jnp.float32)
        * embed_scale
    )
    zeros_row = jnp.zeros((frame_count, 1, width), jnp.float32)
    input_term = jnp.einsum("fd,kde->fke", normed, proj, preferred_element_type=jnp.float32)
    input_term = input_term + jnp.concatenate([zeros_row, looked[:, :-1]], axis=1)
    depth_input = lax.psum(input_term, "tp")
    depth_scale = lax.rsqrt(jnp.mean(depth_input * depth_input, axis=2, keepdims=True) + epsilon)
    depth_hat = depth_input * depth_scale
    depth_normed = (depth_hat * gain_float).astype(jnp.bfloat16)
    triple = jnp.einsum(
        "fke,ecg->fkcg", depth_normed, attn_qkv, preferred_element_type=jnp.float32
    ).astype(jnp.bfloat16)
    attended, attend_back = jax.vjp(attend, triple)
    head_terms = jnp.einsum("fkg,ge->fke", attended, attn_out, preferred_element_type=jnp.float32)
    depth_output = depth_input + lax.psum(head_terms, "tp")
    output_b = depth_output.astype(jnp.bfloat16)
    audio_logits = capped(
        jnp.einsum("fke,kve->fkv", output_b, audio_table, preferred_element_type=jnp.float32)
    )
    audio_sum = jnp.sum(jnp.exp(audio_logits - soft_cap), axis=2)
    audio_chosen = jnp.sum(jnp.where(audio_hot, audio_logits, 0.0), axis=2)
    text_total, text_pick, audio_total, audio_pick = lax.psum(
        (text_sum, text_chosen, audio_sum, audio_chosen), "tp"
    )
    text_lse = soft_cap + jnp.log(text_total)
    audio_lse = soft_cap + jnp.log(audio_total)
    losses = jnp.concatenate([(text_lse - text_pick)[:, None], audio_lse - audio_pick], axis=1)
    text_prob = jnp.exp(text_logits - text_lse[:, None])
    text_grad = ((text_prob - text_hot.astype(jnp.float32)) * cap_slope(text_logits)).astype(
        jnp.bfloat16
    )
    text_back = jnp.dot(text_grad, text_table, preferred_element_type=jnp.float32)
    audio_prob = jnp.exp(audio_logits - audio_lse[:, :, None])
    audio_grad = ((audio_prob - audio_hot.astype(jnp.float32)) * cap_slope(audio_logits)).astype(
        jnp.bfloat16
    )
    vocab_terms = jnp.einsum(
        "fkv,kve->fke", audio_grad, audio_table, preferred_element_type=jnp.float32
    )
    output_back = lax.psum(vocab_terms, "tp")
    output_back_b = output_back.astype(jnp.bfloat16)
    attended_back = jnp.einsum(
        "fke,ge->fkg", output_back_b, attn_out, preferred_element_type=jnp.float32
    ).astype(jnp.bfloat16)
    triple_back = attend_back(attended_back)[0]
    column_terms = jnp.einsum(
        "fkcg,ecg->fke", triple_back, attn_qkv, preferred_element_type=jnp.float32
    )
    normed_back = lax.psum(column_terms, "tp")
    depth_gain_term = jnp.sum(normed_back * depth_hat, axis=(0, 1))
    hat_back = normed_back * gain_float
    input_back = output_back + depth_scale * (
        hat_back - depth_hat * jnp.mean(hat_back * depth_hat, axis=2, keepdims=True)
    )
    input_back_b = input_back.astype(jnp.bfloat16)
    feature_back = lax.psum_scatter(text_back, "tp", scatter_dimension=1, tiled=True)
    feature_back = feature_back + jnp.einsum(
        "fke,kde->fd", input_back_b, proj, preferred_element_type=jnp.float32
    )
    gain_back = feature_back * text_gain.astype(jnp.float32)
    row_dot = lax.psum(jnp.sum(gain_back * hidden_hat, axis=1), "tp")
    grad_hidden = row_scale * (gain_back - hidden_hat * (row_dot[:, None] / D))
    text_gain_term = jnp.sum(feature_back * hidden_hat, axis=0)
    lookup_back = jnp.concatenate([input_back[:, 1:] * embed_scale, zeros_row], axis=1)
    proj_term = jnp.einsum("fd,fke->kde", normed, input_back_b, preferred_element_type=jnp.float32)
    table_term = jnp.einsum(
        "fkv,fke->kve", audio_grad, output_b, preferred_element_type=jnp.float32
    )
    table_term = table_term + jnp.einsum(
        "fkv,fke->kve",
        audio_hot.astype(jnp.float32),
        lookup_back,
        precision=lax.Precision.HIGHEST,
        preferred_element_type=jnp.float32,
    )
    qkv_term = jnp.einsum(
        "fke,fkcg->ecg", depth_normed, triple_back, preferred_element_type=jnp.float32
    )
    out_term = jnp.einsum(
        "fkg,fke->ge", attended, output_back_b, preferred_element_type=jnp.float32
    )
    grad_proj, grad_audio_table, grad_attn_qkv, grad_attn_out = (
        lax.psum_scatter(
            proj_term.astype(jnp.bfloat16), "seq", scatter_dimension=2, tiled=True
        ).astype(jnp.float32),
        lax.psum_scatter(
            table_term.astype(jnp.bfloat16), "seq", scatter_dimension=2, tiled=True
        ).astype(jnp.float32),
        lax.psum_scatter(
            qkv_term.astype(jnp.bfloat16), "seq", scatter_dimension=0, tiled=True
        ).astype(jnp.float32),
        lax.psum_scatter(
            out_term.astype(jnp.bfloat16), "seq", scatter_dimension=1, tiled=True
        ).astype(jnp.float32),
    )
    grad_text_gain, grad_depth_gain = lax.psum((text_gain_term, depth_gain_term), "seq")
    grad_text_table = lax.psum_scatter(
        jnp.einsum("fd,fv->dv", full_normed, text_grad, preferred_element_type=jnp.float32),
        "seq",
        scatter_dimension=0,
        tiled=True,
    )
    return (
        losses,
        grad_hidden,
        grad_text_gain,
        grad_text_table,
        grad_proj,
        grad_audio_table,
        grad_depth_gain,
        grad_attn_qkv,
        grad_attn_out,
    )


def solution(mesh):
    in_specs = (
        P("seq", "tp"),
        P("tp"),
        P("tp", None),
        P(None, "tp", None),
        P(None, "tp", None),
        P(),
        P(None, None, "tp"),
        P("tp", None),
        P("seq"),
        P("seq", None),
    )
    out_specs = (
        P("seq", None),
        P("seq", "tp"),
        P("tp"),
        P("seq", "tp"),
        P(None, "tp", "seq"),
        P(None, "tp", "seq"),
        P(),
        P("seq", None, "tp"),
        P("tp", "seq"),
    )
    return jax.shard_map(
        on_device, mesh=mesh, in_specs=in_specs, out_specs=out_specs, check_vma=False
    )
```

profile of v0, /device:TPU:1, one launch (start us, length us, event | category | flops | bytes accessed | tf_op | source)
XLA Modules:
  0.0 890.9 jit_solution(17193953126050640181)
XLA Ops:
  8.3 34.3 %psum.84 = f32[128]{0:T(128)S(1)} all-reduce(f32[128]{0:T(128)S(1)} %fusion.71), channel_id=1, replica_groups=mesh['seq'=8,'tp'=16] {'tp'}, use_global_device_ids=true, to_apply=%region_1.0 | all-reduce | flops 128 | bytes 1024 | tf_op jit(solution)/shard_map/psum | solution.py:60
  47.1 6.1 pad_add_fusion
  54.1 107.0 %all-reduce.13.cloned.1.call-done = f32[128,8,1024]{2,0,1:T(8,128)} async-done(((f32[128,8,1024]{2,0,1:T(8,128)}), f32[128,8,1024]{2,0,1:T(8,128)}) %all-reduce.13.cloned.1.call-update) | async-done | bytes 4194320 | tf_op jit(solution)/shard_map/psum | solution.py:83
  174.0 31.6 %all-gather.2.cloned.1.call-done = bf16[128,4096]{1,0:T(8,128)(2,1)} async-done(((bf16[128,256]{1,0:T(8,128)(2,1)}), bf16[128,4096]{1,0:T(8,128)(2,1)}) %all-gather.2.cloned.1.call-update) | async-done | bytes 1048592 | tf_op jit(solution)/shard_map/all_gather | solution.py:63
  205.6 5.7 exponential_reduce_fusion
  211.3 101.6 %all-reduce.15.cloned.1.call-done = f32[128,8,1024]{2,0,1:T(8,128)} async-done(((f32[128,8,1024]{2,0,1:T(8,128)}), f32[128,8,1024]{2,0,1:T(8,128)}) %all-reduce.15.cloned.1.call-update) | async-done | bytes 4194320 | tf_op jit(solution)/shard_map/psum | solution.py:92
  312.9 4.2 add_convert_fusion.1
  320.6 32.8 %all-reduce.6 = (f32[128,8]{0,1:T(8,128)S(1)}, f32[128]{0:T(128)}) all-reduce(f32[128,8]{0,1:T(8,128)S(1)} %get-tuple-element.29, f32[128]{0:T(128)} %get-tuple-element.31), channel_id=1, replica_groups=mesh['seq'=8,'tp'=16] {'tp'}, use_global_device_ids=true, to_apply=%region_11.12 | all-reduce | flops 1152 | bytes 9216 | tf_op jit(solution)/shard_map/psum | solution.py:99
  353.4 3.8 convolution_bitcast_fusion.1
  358.1 105.7 %all-reduce.17.cloned.1.call-done = f32[128,8,1024]{2,0,1:T(8,128)} async-done(((f32[128,8,1024]{2,0,1:T(8,128)}), f32[128,8,1024]{2,0,1:T(8,128)}) %all-reduce.17.cloned.1.call-update) | async-done | bytes 4194320 | tf_op jit(solution)/shard_map/psum | solution.py:117
  476.5 3.0 fusion.9
  480.6 6.9 fusion.83
  487.5 88.5 %all-reduce.19.cloned.1.call-done = f32[128,8,1024]{2,0,1:T(8,128)} async-done(((f32[128,8,1024]{2,0,1:T(8,128)}), f32[128,8,1024]{2,0,1:T(8,128)}) %all-reduce.19.cloned.1.call-update) | async-done | bytes 4194320 | tf_op jit(solution)/shard_map/psum | solution.py:126
  576.0 4.7 multiply_reduce_fusion
  590.0 3.4 copy.66
  595.7 5.4 convert_bitcast_fusion
  602.4 8.0 fusion.81
  611.8 27.1 %reduce-scatter.21.cloned.1.call-done = bf16[128,192]{1,0:T(8,128)(2,1)} async-done(((bf16[1024,192]{1,0:T(8,128)(2,1)}), bf16[128,192]{1,0:T(8,128)(2,1)}) %reduce-scatter.21.cloned.1.call-update) | async-done | bytes 49168
  640.5 75.8 %reduce-scatter.13.cloned.1.call-done = f32[128,256]{1,0:T(8,128)} async-done(((f32[128,4096]{1,0:T(8,128)}), f32[128,256]{1,0:T(8,128)}) %reduce-scatter.13.cloned.1.call-update) | async-done | bytes 131088 | tf_op jit(solution)/shard_map/reduce_scatter | solution.py:133
  716.3 5.1 fusion.70
  721.4 15.0 %all-reduce.7 = (f32[256]{0:T(256)}, f32[1024]{0:T(1024)}) all-reduce(f32[256]{0:T(256)S(1)} %get-tuple-element.33, f32[1024]{0:T(1024)S(1)} %get-tuple-element.27), channel_id=1, replica_groups=mesh['seq'=8,'tp'=16] {'seq'}, use_global_device_ids=true, to_apply=%region_22.23 | all-reduce | flops 1280 | bytes 10240 | tf_op jit(solution)/shard_map/psum | solution.py:173
  736.4 31.7 %all-reduce.5 = (f32[128,8]{0,1:T(8,128)S(1)}, f32[128]{0:T(128)S(1)}, f32[128]{0:T(128)S(1)}) all-reduce(f32[128,8]{0,1:T(8,128)S(1)} %copy-done.34, f32[128]{0:T(128)S(1)} %copy-done.35, f32[128]{0:T(128)S(1)} %get-tuple-element.34), channel_id=1, replica_groups=mesh['seq'=8,'tp'=16] {'tp'}, use_global_device_ids=true, to_apply=%region_13.14 | all-reduce | flops 1280 | bytes 10240 | tf_op jit(solution)/shard_map/psum | solution.py:99
  771.6 18.5 %reduce-scatter.17.cloned.1.call-done = bf16[8,256,128]{1,2,0:T(8,128)(2,1)} async-done(((bf16[8,256,1024]{1,2,0:T(8,128)(2,1)}), bf16[8,256,128]{1,2,0:T(8,128)(2,1)}) %reduce-scatter.17.cloned.1.call-update) | async-done | bytes 524304 | tf_op jit(solution)/shard_map/reduce_scatter | solution.py:160
  792.4 92.0 %reduce-scatter.15.cloned.1.call-done = f32[512,1000]{0,1:T(8,128)} async-done(((f32[4096,1000]{0,1:T(8,128)}), f32[512,1000]{0,1:T(8,128)}) %reduce-scatter.15.cloned.1.call-update) | async-done | bytes 2048016 | tf_op jit(solution)/shard_map/reduce_scatter | solution.py:174
  (158 shorter events, 58.6 us)
Async XLA Ops:
  7.2 153.9 %all-reduce.13.cloned.1.call-start = ((), (), s32[]{:S(2)}) async-start(), calls=%async_computation.7 | async-start | bytes 8388608 | tf_op jit(solution)/shard_map/psum | solution.py:83
  7.3 309.8 %copy-start.30 = (s32[128]{0:T(128)}, s32[128]{0:T(128)S(1)}, u32[]{:S(2)}) copy-start(s32[128]{0:T(128)S(1)} %iota_add_fusion.1) | copy-start | bytes 1540
  53.2 110.5 %copy-start.12 = (bf16[1024,3,64]{0,2,1:T(8,128)(2,1)S(1)}, bf16[1024,3,64]{0,2,1:T(8,128)(2,1)}, u32[]{:S(2)}) copy-start(bf16[1024,3,64]{0,2,1:T(8,128)(2,1)} %param.16) | copy-start | bytes 1179652
  53.3 152.3 %all-gather.2.cloned.1.call-start = ((), (), s32[]{:S(2)}) async-start(), calls=%async_computation.6 | async-start | bytes 1114112 | tf_op jit(solution)/shard_map/all_gather | solution.py:63
  54.0 258.8 %all-reduce.15.cloned.1.call-start = ((), (), s32[]{:S(2)}) async-start(), calls=%async_computation.8 | async-start | bytes 8388608 | tf_op jit(solution)/shard_map/psum | solution.py:92
  54.1 114.1 %copy-start.26 = (pred[8,8]{0,1:T(8,128)(4,1)}, pred[8,8]{0,1:T(8,128)(4,1)S(1)}, u32[]{:S(2)}) copy-start(pred[8,8]{0,1:T(8,128)(4,1)S(1)} %iota_compare_fusion) | copy-start | bytes 196
  173.9 289.9 %all-reduce.17.cloned.1.call-start = ((), (), s32[]{:S(2)}) async-start(), calls=%async_computation.10 | async-start | bytes 8388608 | tf_op jit(solution)/shard_map/psum | solution.py:117
  211.3 107.1 %copy-start.25 = (s32[128,8]{0,1:T(8,128)S(1)}, s32[128,8]{0,1:T(8,128)}, u32[]{:S(2)}) copy-start(s32[128,8]{0,1:T(8,128)} %param.19) | copy-start | bytes 12292
  357.2 106.6 %copy-start.24 = (bf16[64,1024]{1,0:T(8,128)(2,1)S(1)}, bf16[64,1024]{1,0:T(8,128)(2,1)}, u32[]{:S(2)}) copy-start(bf16[64,1024]{1,0:T(8,128)(2,1)} %param.17) | copy-start | bytes 393220
  357.2 110.0 %copy-start.10 = (bf16[128,1,8,8]{2,3,0,1:T(8,128)(2,1)S(1)}, bf16[128,1,8,8]{2,3,0,1:T(8,128)(2,1)}, u32[]{:S(2)}) copy-start(bf16[128,1,8,8]{2,3,0,1:T(8,128)(2,1)} %copy-done.9) | copy-start | bytes 49156
  357.3 110.3 %copy-start.27 = (pred[8,8]{0,1:T(8,128)(4,1)S(1)}, pred[8,8]{0,1:T(8,128)(4,1)}, u32[]{:S(2)}) copy-start(pred[8,8]{0,1:T(8,128)(4,1)} %copy-done.26) | copy-start | bytes 196
  357.3 110.6 %copy-start.20 = (bf16[128,8,64]{2,1,0:T(8,128)(2,1)S(1)}, bf16[128,8,64]{2,1,0:T(8,128)(2,1)}, u32[]{:S(2)}) copy-start(bf16[128,8,64]{2,1,0:T(8,128)(2,1)} %copy.40) | copy-start | bytes 393220
  357.3 218.7 %all-reduce.19.cloned.1.call-start = ((), (), s32[]{:S(2)}) async-start(), calls=%async_computation.11 | async-start | bytes 8388608 | tf_op jit(solution)/shard_map/psum | solution.py:126
  358.1 110.8 %copy-start.19 = (bf16[128,8,64]{2,1,0:T(8,128)(2,1)S(1)}, bf16[128,8,64]{2,1,0:T(8,128)(2,1)}, u32[]{:S(2)}) copy-start(bf16[128,8,64]{2,1,0:T(8,128)(2,1)} %copy-done.18) | copy-start | bytes 393220
  472.8 137.5 %reduce-scatter.23.cloned.1.call-start = ((), (), s32[]{:S(2)}) async-start(), calls=%async_computation.16 | async-start | bytes 294912
  476.4 162.5 %reduce-scatter.21.cloned.1.call-start = ((), (), s32[]{:S(2)}) async-start(), calls=%async_computation.15 | async-start | bytes 589824
  480.5 235.8 %reduce-scatter.13.cloned.1.call-start = ((), (), s32[]{:S(2)}) async-start(), calls=%async_computation.9 | async-start | bytes 2228224 | tf_op jit(solution)/shard_map/reduce_scatter | solution.py:133
  487.5 282.0 %reduce-scatter.19.cloned.1.call-start = ((), (), s32[]{:S(2)}) async-start(), calls=%async_computation.14 | async-start | bytes 2359296
  595.4 194.8 %reduce-scatter.17.cloned.1.call-start = ((), (), s32[]{:S(2)}) async-start(), calls=%async_computation.13 | async-start | bytes 4718592 | tf_op jit(solution)/shard_map/reduce_scatter | solution.py:160
  601.2 283.2 %reduce-scatter.15.cloned.1.call-start = ((), (), s32[]{:S(2)}) async-start(), calls=%async_computation.12 | async-start | bytes 18432000 | tf_op jit(solution)/shard_map/reduce_scatter | solution.py:174
  610.3 106.0 %copy-start.17 = (bf16[128,256]{1,0:T(8,128)(2,1)S(1)}, bf16[128,256]{1,0:T(8,128)(2,1)}, u32[]{:S(2)}) copy-start(bf16[128,256]{1,0:T(8,128)(2,1)} %param.10) | copy-start | bytes 196612
  610.3 106.0 %copy-start.33 = (f32[128]{0:T(128)S(1)}, f32[128]{0:T(128)}, u32[]{:S(2)}) copy-start(f32[128]{0:T(128)} %copy-done.32) | copy-start | bytes 1540
  639.9 244.5 %copy-start.1 = (bf16[8,128,1024]{2,1,0:T(8,128)(2,1)S(1)}, bf16[8,128,1024]{2,1,0:T(8,128)(2,1)}, u32[]{:S(2)}) copy-start(bf16[8,128,1024]{2,1,0:T(8,128)(2,1)} %param.14) | copy-start | bytes 6291460
  640.5 95.9 %copy-start.35 = (f32[128]{0:T(128)S(1)}, f32[128]{0:T(128)}, u32[]{:S(2)}) copy-start(f32[128]{0:T(128)} %get-tuple-element.32) | copy-start | bytes 1540
  (25 other events, 240.0 us)
Sparse Core Ops, SparseCore 0:
  53.4 107.6 all-reduce.12
  163.7 41.7 all-gather.1
  208.9 103.8 all-reduce.14
  357.4 106.4 all-reduce.16
  472.9 103.0 all-reduce.18
  578.2 27.7 reduce-scatter.22
  609.1 29.7 reduce-scatter.20
  642.2 74.0 reduce-scatter.12
  718.8 31.7 reduce-scatter.18
  753.0 37.0 reduce-scatter.16
  793.4 90.9 reduce-scatter.14
where the time goes:
time: 892 us; the launch traced here: 891 us
  waiting for transfers between devices  649 us (73%)
  blocking collectives  114 us (13%)
  matrix products  69 us (8%)
  local copies, waits for them, and re-layouts  23.2 us (3%)
  other arithmetic  20.9 us (2%)
  between operations  14.5 us (2%)
    psum x1, waiting for transfers between devices, on_device(): depth_input = lax.psum(input_term, 'tp')  107 us
    psum x1, waiting for transfers between devices, on_device(): output_back = lax.psum(vocab_terms, 'tp')  106 us
    psum x1, waiting for transfers between devices, on_device(): depth_output = depth_input + lax.psum(head_terms, 'tp')  102 us
    reduce_scatter x1, waiting for transfers between devices, on_device(): lax.psum_scatter(jnp.einsum('fd,fv->dv', full_normed, text_grad, preferre...  92 us
    psum x1, waiting for transfers between devices, on_device(): normed_back = lax.psum(column_terms, 'tp')  88.5 us
    reduce_scatter x1, waiting for transfers between devices, on_device(): lax.psum_scatter(text_back, 'tp', scatter_dimension=1, tiled=True)  75.8 us
    psum x2, blocking collectives, on_device(): lax.psum((text_sum, text_chosen, audio_sum, audio_chosen), 'tp')  64.5 us
    psum x1, blocking collectives, on_device(): squares = lax.psum(jnp.sum(hidden_float * hidden_float, axis=1), 'tp')  34.3 us
  transfers between devices with their start and end apart: 11, of which 9 were waited for; matrix products, arithmetic and copies ran while one was open for 9% of the time, Pallas kernels for 0%

commit v1 on v0

v1 whole, which is shorter than its diff:
```python
import math

import jax
import jax.numpy as jnp
from jax import lax
from jax.experimental import pallas as pl
from jax.experimental.pallas import tpu as pltpu
from jax.sharding import Mesh
from jax.sharding import PartitionSpec as P

D = 4096
DD = 1024
HEAD = 64
VOCAB = 1000
MESH = pl.DeviceIdType.MESH
VMEM_LIMIT = 62 * 1024 * 1024

soft_cap = 12.0
epsilon = 1e-05
embed_scale = math.sqrt(DD) / 4.0
f32 = jnp.float32
bf16 = jnp.bfloat16

NN = (((1,), (0,)), ((), ()))
NT = (((1,), (1,)), ((), ()))
TN = (((0,), (0,)), ((), ()))


def dot(a, b, dims=NN):
    return lax.dot_general(a, b, dims, preferred_element_type=f32)


def capped(values):
    return soft_cap * jnp.tanh(values / soft_cap)


def cap_slope(capped_values):
    ratio = capped_values / soft_cap
    return 1.0 - ratio * ratio


class Place:
    def __init__(self):
        self.z = lax.axis_index("z")
        self.c = lax.axis_index("core")
        self.x = lax.axis_index("x")
        self.y = lax.axis_index("y")
        self.s = self.z * 2 + self.c
        self.t = self.x * 4 + self.y

    def ring(self, axis):
        me = {"x": self.x, "y": self.y, "z": self.z}[axis]
        return me, lax.rem(me + 1, 4), lax.rem(me + 2, 4), lax.rem(me + 3, 4)

    def xp(self, d):
        to = lax.rem(self.x + d, 4)
        return to, {"x": to}

    def yp(self, d):
        to = lax.rem(self.y + d, 4)
        return to, {"y": to}

    def sp(self, d):
        to = lax.rem(self.s + d, 8)
        return to, {"z": lax.div(to, 2), "core": lax.rem(to, 2)}

    def tp(self, d):
        to = lax.rem(self.t + d, 16)
        return to, {"x": lax.div(to, 4), "y": lax.rem(to, 4)}

    def sibling(self):
        return {"core": 1 - self.c}


class Sends:
    def __init__(self, at):
        self.at = at
        self.pending = []

    def go(self, src, dst, send, recv, device):
        pltpu.make_async_remote_copy(
            src_ref=src, dst_ref=dst, send_sem=send, recv_sem=recv, device_id=device, device_id_type=MESH
        ).start()

    def bytes_of(self, ref, sem):
        return pltpu.make_async_remote_copy(
            src_ref=ref, dst_ref=ref, send_sem=sem, recv_sem=sem,
            device_id=self.at.sibling(), device_id_type=MESH,
        )

    def sent_later(self, ref, sem):
        self.pending.append(self.bytes_of(ref, sem))

    def one(self, src, dst, sems, device):
        self.go(src, dst, sems.at[0], sems.at[1], device)
        self.sent_later(src, sems.at[0])
        return self.bytes_of(dst, sems.at[1])

    def spread(self, peer, n, src, dst, sems, slots, all_bytes=None):
        for d in range(1, n):
            to, device = peer(d)
            self.go(src(to), dst, sems.at[0], sems.at[1], device)
        if all_bytes is None:
            all_bytes = slots.at[pl.ds(0, n - 1)]
        self.sent_later(all_bytes, sems.at[0])
        return self.bytes_of(all_bytes, sems.at[1])

    def finish(self):
        for wait in self.pending:
            wait.wait_send()


class RingGather:
    def __init__(self, out, at, axis, part, slots, sems):
        self.out, self.part, self.sems, self.slots = out, part, sems, slots
        me, self.right, far, self.left = at.ring(axis)
        self.to_right, self.to_left = {axis: self.right}, {axis: self.left}
        block = part(me, None)
        out.go(block, block, sems.at[0], sems.at[1], self.to_right)
        out.go(block, block, sems.at[0], sems.at[2], self.to_left)
        out.sent_later(slots(3), sems.at[0])

    def forward(self):
        out, part, sems = self.out, self.part, self.sems
        out.bytes_of(part(self.left, None), sems.at[1]).wait_recv()
        one = part(self.left, 0)
        out.go(one, one, sems.at[0], sems.at[3], self.to_right)
        out.bytes_of(part(self.right, None), sems.at[2]).wait_recv()
        two = part(self.right, 1)
        out.go(two, two, sems.at[0], sems.at[3], self.to_left)

    def finish(self):
        self.out.bytes_of(self.slots(1), self.sems.at[3]).wait_recv()


class RingReduce:
    def __init__(self, out, at, axis, blocks, half, bufs, sems):
        self.out, self.half, self.sems, self.blocks = out, half, sems, blocks
        self.me, self.right, far, self.left = at.ring(axis)
        self.rl, self.rr, self.fa, self.fb = bufs
        self.to_right, self.to_left = {axis: self.right}, {axis: self.left}
        s = blocks
        out.go(half(s.at[far], 0), self.fa, sems.at[0], sems.at[1], self.to_right)
        out.go(half(s.at[far], 1), self.fb, sems.at[0], sems.at[2], self.to_left)
        out.go(half(s.at[self.right], 1), half(self.rl, 1), sems.at[0], sems.at[3], self.to_right)
        out.go(half(s.at[self.left], 0), half(self.rr, 0), sems.at[0], sems.at[3], self.to_left)
        out.sent_later(s.at[pl.ds(0, 3)], sems.at[0])

    def forward(self):
        s, half, out, sems = self.blocks, self.half, self.out, self.sems
        out.bytes_of(self.fa, sems.at[1]).wait_recv()
        one = half(s.at[self.right], 0)
        one[...] = (one[...].astype(f32) + self.fa[...].astype(f32)).astype(bf16)
        out.go(one, half(self.rl, 0), sems.at[0], sems.at[3], self.to_right)
        out.bytes_of(self.fb, sems.at[2]).wait_recv()
        two = half(s.at[self.left], 1)
        two[...] = (two[...].astype(f32) + self.fb[...].astype(f32)).astype(bf16)
        out.go(two, half(self.rr, 1), sems.at[0], sems.at[3], self.to_left)

    def finish(self):
        self.out.bytes_of(self.blocks.at[pl.ds(0, 2)], self.sems.at[3]).wait_recv()

    def total(self, pick=lambda ref: ref[...]):
        own = pick(self.blocks.at[self.me]).astype(f32)
        return own + pick(self.rl).astype(f32) + pick(self.rr).astype(f32)


class DirectReduce:
    def __init__(self, out, at, axis, blocks, got, sems):
        self.blocks, self.got = blocks, got
        self.me = at.ring(axis)[0]
        for d in (2, 1, 3):
            to = lax.rem(self.me + d, 4)
            out.go(blocks.at[to], got.at[d - 1], sems.at[0], sems.at[1], {axis: to})
        out.sent_later(blocks.at[pl.ds(0, 3)], sems.at[0])
        self.wait = out.bytes_of(got, sems.at[1])

    def finish(self):
        self.wait.wait_recv()

    def total(self, pick=lambda ref: ref[...]):
        own = pick(self.blocks.at[self.me]).astype(f32)
        for d in range(3):
            own = own + pick(self.got.at[d]).astype(f32)
        return own


def span(h, size):
    if h is None:
        return pl.ds(0, size)
    return pl.ds(h * (size // 2), size // 2)


def rows_half(n):
    return lambda ref, h: ref.at[pl.ds(h * n, n)]


def row_to_col(row, lanes):
    return jnp.broadcast_to(row, (lanes, row.shape[1])).T


def twice(col):
    return jnp.concatenate([col, col], axis=1)


def fold(rows, n):
    w = rows.shape[1] // n
    return jnp.concatenate([rows[:, i * w : i * w + w] for i in range(n)], axis=0).astype(bf16)


def unfold(packed, n):
    r = packed.shape[0] // n
    wide = packed.astype(f32)
    return jnp.concatenate([wide[i * r : i * r + r] for i in range(n)], axis=1)


def by_step(rows):
    return [fold(rows[4 * k : 4 * k + 4], 4) for k in range(8)]


def from_steps(ref):
    return jnp.concatenate([unfold(ref[k], 4) for k in range(8)], axis=0)


def head_masks(rows):
    lane = lax.broadcasted_iota(jnp.int32, (rows, 256), 1)
    return [(lane >= 64 * h) & (lane < 64 * h + 64) for h in range(4)]


def step_mask():
    i = lax.broadcasted_iota(jnp.int32, (128, 128), 0)
    j = lax.broadcasted_iota(jnp.int32, (128, 128), 1)
    return ((i & 3) == (j & 3)) & ((i >> 5) == (j >> 5)) & (j <= i)


def attention(qh, kk, allowed):
    scores = dot(qh, kk, NT) / math.sqrt(HEAD)
    raised = jnp.where(allowed, jnp.exp(scores), 0.0)
    return raised / jnp.sum(raised, axis=1, keepdims=True)


def ring_reduce_scratch(name, block, half):
    return [
        (name + "_s", (4,) + block, bf16),
        (name + "_rl", block, bf16),
        (name + "_rr", block, bf16),
        (name + "_fa", half, bf16),
        (name + "_fb", half, bf16),
        (name + "_m", 4, None),
    ]


def direct_scratch(name, block):
    return [(name + "_s", (4,) + block, bf16), (name + "_r", (3,) + block, bf16), (name + "_m", 2, None)]


def chain_scratch(m):
    m = str(m)
    return [
        *ring_reduce_scratch("p" + m, (4, 16, DD), (2, 16, DD)),
        *ring_reduce_scratch("q" + m, (4, 16, DD), (2, 16, DD)),
        *direct_scratch("pp" + m, (16, DD)),
        *direct_scratch("qq" + m, (16, DD)),
        ("dn_m" + m, 2, None),
        *direct_scratch("h" + m, (32, DD)),
        ("a1s" + m, (8, 16, 256), bf16), ("a1r" + m, (8, 16, 256), bf16), ("a1_m" + m, 2, None),
        ("a2s" + m, (8, 16, 256), bf16), ("a2r" + m, (8, 16, 256), bf16), ("a2_m" + m, 2, None),
        ("a3s" + m, (8, 16, 256), bf16), ("a3r" + m, (8, 16, 256), bf16), ("a3_m" + m, 2, None),
        ("ob_m" + m, 2, None), ("e" + m, (4, 8, 128), f32), ("e_m" + m, 2, None),
        *direct_scratch("v" + m, (32, DD)),
        *direct_scratch("c" + m, (32, DD)),
        ("obb_m" + m, 2, None),
    ]


SCRATCH = [
    ("tt", (VOCAB, D), bf16), ("pj", (8, 256, DD), bf16), ("au", (8, 128, DD), bf16), ("load", 3, 0),
    ("ssq", (16, 8, 128), f32), ("ssq_m", 2, None),
    ("idb", (8, 8, 128), jnp.int32), ("idb_m", 2, None), ("idr", (2, 1, 1024), jnp.int32),
    ("raw", (8, 128, DD), f32), ("look", (8, 128, DD), bf16),
    ("wb", (4, 4, 64, DD), bf16), ("wb_m", 4, None), ("wz_m", 4, None), ("wc_m", 2, None),
    ("nb", (4, 4, 128, 256), bf16), ("ny_m", 4, None), ("nx_m", 4, None),
    ("ns", (4, 2, 16, 16, 128), bf16), ("nz_m", 4, None), ("nc_m", 2, None),
    *chain_scratch(0), *chain_scratch(1),
    ("dob", (2, 2, 4, 32, DD), bf16), ("qkv", (2, 3, 128, 256), bf16),
    ("ex", (2, 4, 128, 128), f32), ("ob", (2, 4, 32, DD), bf16),
    ("gr", (2, 128, 512), bf16), ("tri", (2, 4, 128, 256), bf16),
    ("tab", (4, 128, DD), bf16), ("tab_m", 4, None),
    ("tl", (128, VOCAB), f32), ("ts", (16, 8, 128), f32), ("ts_m", 2, None), ("tgr", (128, VOCAB), bf16),
    *ring_reduce_scratch("g", (128, DD), (64, DD)),
    ("lc", (8, 2, 16, 128), f32), ("lr", (8, 2, 16, 128), f32), ("lc_m", 2, None),
    ("lx", (4, 2, 16, 128), f32), ("lx_m", 2, None), ("tlc", (128, 128), f32),
    ("nt", (256, 1024), bf16), ("tg", (4, 2, 1024, 128), bf16), ("tgz_m", 4, None), ("tgc_m", 2, None),
    *ring_reduce_scratch("t", (4, 128, 256), (2, 128, 256)),
    *ring_reduce_scratch("t2", (128, 256), (64, 256)),
    ("ndst", (8, 2, 128, 256), bf16), ("nd_m", 2, None),
    ("ib", (2, 4, 4, 32, DD), bf16), ("i0x_m", 2, None), ("i0y_m", 4, None),
    ("iax_m", 2, None), ("iay_m", 4, None), ("ibx_m", 4, None), ("iby_m", 2, None),
    ("gas", (2, 4, 4, 64, 512), bf16), ("gar", (4, 4, 64, 512), bf16), ("gar_m", 2, None),
    *ring_reduce_scratch("ga", (4, 64, 512), (2, 64, 512)),
    *direct_scratch("gz", (4, 64, 128)),
    ("sf", (2, 4, 128, 256), bf16), ("sfr", (4, 128, 256), bf16), ("sfr_m", 2, None),
    *direct_scratch("f", (128, 256)),
    ("gps", (8, 256, 128), bf16), ("gpr", (8, 256, 128), bf16), ("gp_m", 2, None),
    ("lks", (8, 128, 128), bf16), ("lkr", (8, 128, 128), bf16), ("lk_m", 2, None),
    ("gts", (8, 128, 128), bf16), ("gtr", (8, 128, 128), bf16), ("gt_m", 2, None),
    ("dgs", (8, 8, 128), f32), ("dgs_m", 2, None), ("dgt", (16, 8, 128), f32), ("dgt_m", 2, None),
    ("rd", (16, 8, 128), f32), ("rd_m", 2, None), ("tgn", (8, 8, 256), f32), ("tgn_m", 2, None),
]


def scratch_shape(entry):
    name, shape, dtype = entry
    if dtype is None or isinstance(dtype, int):
        return pltpu.SemaphoreType.DMA((shape,))
    return pltpu.VMEM(shape, dtype)


class Named:
    pass


def loop(low, high, body):
    def one(i, carry):
        body(i)
        return carry

    lax.fori_loop(low, high, one, 0)


INPUTS = ["hid", "gain", "table", "proj", "audio", "dgain", "wqkv", "wout", "tid", "ids"]
OUTPUTS = ["o_loss", "o_gh", "o_tgain", "o_gtt", "o_gp", "o_gtab", "o_dg", "o_gqkv", "o_gout"]


def kernel(*refs):
    n = Named()
    names = INPUTS + OUTPUTS + [entry[0] for entry in SCRATCH]
    for name, ref in zip(names, refs):
        setattr(n, name, ref)
    at = Place()
    out = Sends(at)

    def reduce(axis, name, half):
        bufs = [getattr(n, name + suffix) for suffix in ("_rl", "_rr", "_fa", "_fb")]
        return RingReduce(out, at, axis, getattr(n, name + "_s"), half, bufs, getattr(n, name + "_m"))

    def direct(axis, name):
        return DirectReduce(
            out, at, axis, getattr(n, name + "_s"), getattr(n, name + "_r"), getattr(n, name + "_m")
        )

    def seq_all(src, dst, sems):
        return out.spread(at.sp, 8, lambda to: src.at[to], dst.at[at.s], sems, dst)

    def seq_same(ref, sems):
        return out.spread(at.sp, 8, lambda to: ref.at[at.s], ref.at[at.s], sems, ref)

    def plane_same(ref, sems):
        return out.spread(at.tp, 16, lambda to: ref.at[at.t], ref.at[at.t], sems, ref)

    def x_same(ref, sems):
        return out.spread(at.xp, 4, lambda to: ref.at[at.x], ref.at[at.x], sems, ref)

    def y_same(ref, sems):
        return out.spread(at.yp, 4, lambda to: ref.at[at.y], ref.at[at.y], sems, ref)

    loads = [
        pltpu.make_async_copy(src, dst, n.load.at[i])
        for i, (src, dst) in enumerate([(n.proj, n.pj), (n.audio, n.au), (n.table, n.tt)])
    ]
    for copy in loads:
        copy.start()
    for c in range(3):
        n.wb[at.x, c] = n.wqkv[c]
    n.wb[at.x, 3] = n.wout[...]
    barrier = pltpu.get_barrier_semaphore()
    for d in range(1, 16):
        pl.semaphore_signal(barrier, inc=1, device_id=at.tp(d)[1], device_id_type=MESH)
    for d in range(1, 8):
        pl.semaphore_signal(barrier, inc=1, device_id=at.sp(d)[1], device_id_type=MESH)
    h = n.hid[...].astype(f32)
    gain = n.gain[...].astype(f32)[None, :]
    dgain = n.dgain[...].astype(f32)[None, :]
    ones = jnp.ones((8, 256), f32)
    n.ssq[at.t] = lax.dot_general(
        ones, h * h, NT, precision=lax.Precision.HIGHEST, preferred_element_type=f32
    )
    n.idb[at.s] = n.ids[...]
    unscaled = (h * gain).astype(bf16)
    pl.semaphore_wait(barrier, 22)

    got_ssq = plane_same(n.ssq, n.ssq_m)
    mine = pl.ds(pl.multiple_of(at.c * 32, 32), 32)
    weights = RingGather(
        out, at, "x",
        lambda i, hf: n.wb.at[i, at.z, mine] if hf is None
        else n.wb.at[i, at.z, pl.ds(pl.multiple_of(at.c * 32 + 16 * hf, 16), 16)],
        lambda k: n.wb.at[pl.ds(0, k), at.z, mine],
        n.wb_m,
    )
    got_ids = seq_same(n.idb, n.idb_m)
    loads[0].wait()

    def raw_step(k):
        n.raw[k] = dot(unscaled, n.pj[k])

    loop(0, 8, raw_step)
    loads[1].wait()
    entry = (lax.broadcasted_iota(jnp.int32, (128, 128), 1) + at.t * 128).astype(f32)
    n.look[0] = jnp.zeros((128, DD), bf16)

    def look_step(k):
        column = row_to_col(n.ids[pl.ds(k, 1), :].astype(f32), 128)
        hot = jnp.where(column == entry, 1.0, 0.0).astype(bf16)
        n.look[k + 1] = (dot(hot, n.au[k]) * embed_scale).astype(bf16)

    loop(0, 7, look_step)
    got_ssq.wait_recv()
    scale = row_to_col(lax.rsqrt(jnp.sum(n.ssq[...], axis=0)[0:1, :] / D + epsilon), 128)
    column = scale[:, 0:1]
    scale = twice(scale)
    hat = h * scale

    first = []
    for m in range(2):
        ps, qs = getattr(n, f"p{m}_s"), getattr(n, f"q{m}_s")
        part = slice(64 * m, 64 * m + 64)

        def scaled(k):
            return n.raw[k, part, :] * column[part] + n.look[k, part, :].astype(f32)

        def to_x(k):
            p = scaled(k)
            for b in range(4):
                ps[b, k] = p[16 * b : 16 * b + 16].astype(bf16)

        def to_y(k):
            p = scaled(k + 4)
            for b in range(4):
                rows = [p[16 * a + 4 * b : 16 * a + 4 * b + 4] for a in range(4)]
                qs[b, k] = jnp.concatenate(rows, axis=0).astype(bf16)

        loop(0, 4, to_x)
        red_p = reduce("x", f"p{m}", rows_half(2))
        loop(0, 4, to_y)
        first.append((red_p, reduce("y", f"q{m}", rows_half(2))))
    normed_f = hat * gain
    n.nb[at.x, at.y] = normed_f.astype(bf16)
    for b in range(16):
        n.ns[at.z, at.c, b] = fold(normed_f[8 * b : 8 * b + 8], 2)
    norm_z = RingGather(
        out, at, "z",
        lambda i, hf: n.ns.at[i, at.c, span(hf, 16)],
        lambda k: n.ns.at[pl.ds(0, k), at.c],
        n.nz_m,
    )
    norm_y = RingGather(
        out, at, "y",
        lambda i, hf: n.nb.at[at.x, i, span(hf, 128)],
        lambda k: n.nb.at[at.x, pl.ds(0, k)],
        n.ny_m,
    )

    masks = head_masks(128)
    allowed = step_mask()
    held = [Named(), Named()]

    def wcat(c):
        return jnp.concatenate([n.wb[a, c] for a in range(4)], axis=0)

    def half_of(m, name):
        return getattr(n, name + str(m))

    def chain(m):
        mine = held[m]
        red_p, red_q = first[m]
        red_p.forward()
        red_q.forward()
        yield
        for red, to, axis in ((red_p, "pp", "y"), (red_q, "qq", "x")):
            red.finish()
            total = [red.total(lambda ref: ref[k]) for k in range(4)]
            for b in range(4):
                rows = [total[k][4 * b : 4 * b + 4] for k in range(4)]
                getattr(n, f"{to}{m}_s")[b] = jnp.concatenate(rows, axis=0).astype(bf16)
            if axis == "y":
                red_pp = direct("y", f"pp{m}")
            else:
                red_qq = direct("x", f"qq{m}")
        yield
        red_pp.finish()
        red_qq.finish()
        di = jnp.concatenate([red_pp.total(), red_qq.total()], axis=0)
        mine.dscale = lax.rsqrt(jnp.mean(di * di, axis=1, keepdims=True) + epsilon)
        mine.dhat = di * mine.dscale
        n.dob[0, m, at.y] = (mine.dhat * dgain).astype(bf16)
        got = y_same(n.dob.at[0, m], half_of(m, "dn_m"))
        yield
        got.wait_recv()
        dnv = n.dob[0, m].reshape(128, DD)
        for c in range(3):
            n.qkv[m, c] = dot(dnv, wcat(c), NT).astype(bf16)
        q, k, v = n.qkv[m, 0], n.qkv[m, 1], n.qkv[m, 2]
        mixed = jnp.zeros((128, 256), f32)
        for hd in range(4):
            qh = jnp.where(masks[hd], q, jnp.zeros_like(q))
            exact = attention(qh, k, allowed)
            n.ex[m, hd] = exact
            mixed = jnp.where(masks[hd], dot(exact.astype(bf16), v), mixed)
        n.tri[m, 3] = mixed.astype(bf16)
        terms = dot(n.tri[m, 3], wcat(3))
        for b in range(4):
            getattr(n, f"h{m}_s")[b] = terms[32 * b : 32 * b + 32].astype(bf16)
        red_h = direct("y", f"h{m}")
        yield
        red_h.finish()
        src, dst = half_of(m, "a1s"), half_of(m, "a1r")
        for k, block in enumerate(by_step(di + red_h.total())):
            src[k] = block
        got = seq_all(src, dst, half_of(m, "a1_m"))
        dst[at.s] = src[at.s]
        yield
        got.wait_recv()
        n.ob[m, at.y] = from_steps(dst).astype(bf16)
        got = y_same(n.ob.at[m], half_of(m, "ob_m"))
        yield
        got.wait_recv()
        rows = n.ob[m].reshape(128, DD)
        tab = n.tab[...].reshape(512, DD)
        logits = capped(dot(rows, tab, NT))
        hot = mine.hot
        sums = jnp.sum(jnp.exp(logits - soft_cap), axis=1, keepdims=True)
        chosen = jnp.sum(jnp.where(hot, logits, 0.0), axis=1, keepdims=True)
        lane = lax.broadcasted_iota(jnp.int32, (128, 128), 1)
        packed = jnp.where(lane == 0, sums, jnp.where(lane == 1, chosen, 0.0))
        e = half_of(m, "e")
        e[at.y] = packed.T[0:8, :]
        got = y_same(e, half_of(m, "e_m"))
        yield
        got.wait_recv()
        total = jnp.sum(e[...], axis=0)
        lse_row = soft_cap + jnp.log(total[0:1, :])
        prob = jnp.exp(logits - row_to_col(lse_row, 128)[:, 0:1])
        grad = ((prob - jnp.where(hot, 1.0, 0.0)) * cap_slope(logits)).astype(bf16)
        n.gr[m] = grad
        terms = dot(grad, tab)
        for b in range(4):
            getattr(n, f"v{m}_s")[b] = terms[32 * b : 32 * b + 32].astype(bf16)
        red_v = direct("y", f"v{m}")
        loss = row_to_col(lse_row - total[1:2, :], 128)
        for g in range(8):
            rows = [loss[32 * b + 4 * g : 32 * b + 4 * g + 4] for b in range(4)]
            n.lc[g, m] = jnp.concatenate(rows, axis=0)
        yield
        red_v.finish()
        src, dst = half_of(m, "a2s"), half_of(m, "a2r")
        for k, block in enumerate(by_step(red_v.total())):
            src[k] = block
        got = seq_all(src, dst, half_of(m, "a2_m"))
        dst[at.s] = src[at.s]
        yield
        got.wait_recv()
        output_back = from_steps(dst)
        n.dob[1, m, at.y] = output_back.astype(bf16)
        got = y_same(n.dob.at[1, m], half_of(m, "obb_m"))
        yield
        got.wait_recv()
        g = dot(n.dob[1, m].reshape(128, DD), wcat(3), NT).astype(bf16)
        q, k, v = n.qkv[m, 0], n.qkv[m, 1], n.qkv[m, 2]
        dq = jnp.zeros((128, 256), f32)
        dk = jnp.zeros((128, 256), f32)
        dv = jnp.zeros((128, 256), f32)
        for hd in range(4):
            gh = jnp.where(masks[hd], g, jnp.zeros_like(g))
            exact = n.ex[m, hd]
            dw = dot(gh, v, NT).astype(bf16).astype(f32)
            ds = exact * (dw - jnp.sum(dw * exact, axis=1, keepdims=True)) / math.sqrt(HEAD)
            dv = jnp.where(masks[hd], dot(exact.T.astype(bf16), g), dv)
            dq = jnp.where(masks[hd], dot(ds.astype(bf16), k), dq)
            dk = jnp.where(masks[hd], dot(ds.T.astype(bf16), q), dk)
        n.tri[m, 0] = dq.astype(bf16)
        n.tri[m, 1] = dk.astype(bf16)
        n.tri[m, 2] = dv.astype(bf16)
        terms = dot(n.tri[m, 0], wcat(0)) + dot(n.tri[m, 1], wcat(1)) + dot(n.tri[m, 2], wcat(2))
        for b in range(4):
            getattr(n, f"c{m}_s")[b] = terms[32 * b : 32 * b + 32].astype(bf16)
        red_c = direct("y", f"c{m}")
        yield
        red_c.finish()
        nback = red_c.total()
        mine.gain_term = jnp.sum(nback * mine.dhat, axis=0, keepdims=True)
        hback = nback * dgain
        inner = jnp.mean(hback * mine.dhat, axis=1, keepdims=True)
        ib = output_back + mine.dscale * (hback - mine.dhat * inner)
        src, dst = half_of(m, "a3s"), half_of(m, "a3r")
        for k, block in enumerate(by_step(ib)):
            src[k] = block
        got = seq_all(src, dst, half_of(m, "a3_m"))
        dst[at.s] = src[at.s]
        yield
        got.wait_recv()
        n.ib[m, at.x, at.y] = from_steps(dst).astype(bf16)

        def part(axis, where, sems):
            return RingGather(out, at, axis, where, lambda k: where(pl.ds(0, k), None), sems)

        def spread(peer, mine_is, where, sems):
            src = where(mine_is)
            return out.spread(peer, 4, lambda to: src, src, sems, None, where(pl.ds(0, 3)))

        low, high = pl.ds(0, 16), pl.ds(16, 16)
        ib = n.ib.at[m]
        if m == 0:
            one = [spread(at.xp, at.x, lambda i: ib.at[i, at.y], n.i0x_m)]
        else:
            one = [
                spread(at.xp, at.x, lambda i: ib.at[i, at.y, low], n.iax_m),
                spread(at.yp, at.y, lambda i: ib.at[at.x, i, high], n.iby_m),
            ]
        yield
        one[0].wait_recv()
        if m == 0:
            two = [part("y", lambda i, hf: ib.at[:, i, :, span(hf, DD)], n.i0y_m)]
        else:
            two = [part("y", lambda i, hf: ib.at[:, i, low, span(hf, DD)], n.iay_m)]
            one[1].wait_recv()
            two.append(part("x", lambda i, hf: ib.at[i, :, high, span(hf, DD)], n.ibx_m))
        yield
        for ring in two:
            ring.forward()
        yield
        for ring in two:
            ring.finish()
        yield

    run = [chain(0), chain(1)]

    def step(m):
        next(run[m])

    def text_piece(i):
        feats = jnp.concatenate([n.nb[i // 2, 2 * (i % 2) + b] for b in range(2)], axis=1)
        part = dot(feats, n.tt[:, 512 * i : 512 * i + 512], NT)
        if i == 0:
            n.tl[...] = part
        else:
            n.tl[...] += part

    def text_back(a):
        part = dot(n.tgr[...], n.tt[:, 1024 * a : 1024 * a + 1024])
        for b in range(4):
            n.t_s[a, b] = part[:, 256 * b : 256 * b + 256].astype(bf16)

    weights.forward()
    step(0)
    step(1)
    norm_y.forward()
    weights.finish()
    weights_z = RingGather(
        out, at, "z",
        lambda i, hf: n.wb.at[span(hf, 4), i, mine],
        lambda k: n.wb.at[:, pl.ds(0, k), mine],
        n.wz_m,
    )
    step(0)
    norm_z.forward()
    norm_y.finish()
    norm_x = RingGather(
        out, at, "x", lambda i, hf: n.nb.at[i, span(hf, 4)], lambda k: n.nb.at[pl.ds(0, k)], n.nx_m
    )
    step(1)
    weights_z.forward()
    step(0)
    n.tab[at.x] = n.au[at.s]
    tab_x = RingGather(
        out, at, "x", lambda i, hf: n.tab.at[i, span(hf, 128)], lambda k: n.tab.at[pl.ds(0, k)], n.tab_m
    )
    step(1)
    norm_z.finish()
    share = n.ns.at[:, at.c]
    wait_n = out.one(share, share, n.nc_m, at.sibling())
    weights_z.finish()
    for other in (weights.right, lax.rem(at.x + 2, 4), weights.left):
        part = n.wb.at[other, :, mine]
        out.go(part, part, n.wc_m.at[0], n.wc_m.at[1], at.sibling())
    out.sent_later(n.wb.at[pl.ds(0, 3), :, mine], n.wc_m.at[0])
    wait_w = out.bytes_of(n.wb.at[pl.ds(0, 3), :, mine], n.wc_m.at[1])
    got_ids.wait_recv()
    i = lax.broadcasted_iota(jnp.int32, (128, 1024), 0)
    j = lax.broadcasted_iota(jnp.int32, (128, 1024), 1)
    same = ((i >> 6) == (j >> 9)) & (((i >> 2) & 15) == ((j >> 5) & 15)) & ((i & 3) == (j & 3))
    group = lax.broadcasted_iota(jnp.int32, (8, 1024), 0)
    j = lax.broadcasted_iota(jnp.int32, (8, 1024), 1)
    book = [at.s, jnp.maximum(at.s - 1, 0)]
    ids2 = [jnp.concatenate([n.idb[g, pl.ds(k, 1), :] for g in range(8)], axis=0) for k in book]
    spread = lax.dot_general(
        jnp.concatenate(ids2, axis=0).astype(f32), jnp.where(same, 1.0, 0.0), NN,
        precision=lax.Precision.HIGHEST, preferred_element_type=f32,
    )
    for i in range(2):
        own = jnp.where(((j >> 2) & 7) == group, spread[8 * i : 8 * i + 8], 0.0)
        n.idr[i] = jnp.sum(own, axis=0, keepdims=True).astype(jnp.int32)
    norm_x.forward()
    wait_w.wait_recv()
    step(0)
    step(1)
    wait_n.wait_recv()
    def transposed(b):
        rows = []
        for t in range(4):
            for s in range(8):
                index = 8 * lax.div(b, 4) + 2 * lax.rem(b, 4) + t // 2
                tile = unfold(n.ns[s // 2, s % 2, index], 2)
                rows.append(tile[4 * (t % 2) : 4 * (t % 2) + 4])
        cols = pl.ds(pl.multiple_of(128 * b, 128), 128)
        n.nt[:, cols] = jnp.concatenate(rows, axis=0).T.astype(bf16)

    loop(0, 8, transposed)
    step(0)
    tab_x.forward()
    step(1)
    norm_x.finish()
    loads[2].wait()
    text_piece(0)
    text_piece(1)
    step(0)
    text_piece(2)
    step(1)
    def two_blocks(to):
        return n.nb.at[lax.div(to, 2), pl.ds(2 * lax.rem(to, 2), 2)]

    n.ndst[at.s] = two_blocks(at.s)[...]
    got_nd = out.spread(at.sp, 8, two_blocks, n.ndst.at[at.s], n.nd_m, n.ndst)
    for m in range(2):
        row = n.idr[0, :, pl.ds(pl.multiple_of(at.x * 128 + 512 * m, 128), 128)]
        local = jnp.where(((row >> 7) & 3) == at.y, ((row >> 9) << 7) | (row & 127), -1)
        column = row_to_col(local.astype(f32), 128)[:, 0:1]
        held[m].hot = column == lax.broadcasted_iota(jnp.int32, (128, 512), 1).astype(f32)
    tab_x.finish()
    text_piece(3)
    step(0)
    step(1)
    text_piece(4)
    step(0)
    text_piece(5)
    step(1)
    text_piece(6)
    text_piece(7)
    step(0)
    step(1)
    tl = capped(n.tl[...])
    n.tl[...] = tl
    tid = row_to_col(n.tid[...].astype(f32), 128)[:, 0:1]
    text_hot = tid == lax.broadcasted_iota(jnp.int32, (128, VOCAB), 1).astype(f32) + (at.t * VOCAB).astype(f32)
    tsum = jnp.sum(jnp.exp(tl - soft_cap), axis=1, keepdims=True)
    tchosen = jnp.sum(jnp.where(text_hot, tl, 0.0), axis=1, keepdims=True)
    lane = lax.broadcasted_iota(jnp.int32, (128, 128), 1)
    packed = jnp.where(lane == 0, tsum, jnp.where(lane == 1, tchosen, 0.0))
    n.ts[at.t] = packed.T[0:8, :]
    got_ts = plane_same(n.ts, n.ts_m)
    step(0)
    def vocab_grad(b):
        part = n.gr[:, :, pl.ds(pl.multiple_of(128 * b, 128), 128)].reshape(256, 128)
        n.g_s[b] = dot(part.astype(f32).T.astype(bf16), n.ob[...].reshape(256, DD)).astype(bf16)

    loop(0, 4, vocab_grad)
    red_g = reduce("x", "g", rows_half(64))
    step(1)
    got_lc = seq_all(n.lc, n.lr, n.lc_m)
    n.lr[at.s] = n.lc[at.s]
    got_ts.wait_recv()
    ttotal = jnp.sum(n.ts[...], axis=0)
    tlse_row = soft_cap + jnp.log(ttotal[0:1, :])
    n.tlc[...] = row_to_col(tlse_row - ttotal[1:2, :], 128)
    tl = n.tl[...]
    tgrad = jnp.exp(tl - row_to_col(tlse_row, 128)[:, 0:1]) - jnp.where(text_hot, 1.0, 0.0)
    tgrad = tgrad * cap_slope(tl)
    n.tgr[...] = tgrad.astype(bf16)
    step(0)
    padded = jnp.concatenate([tgrad, jnp.zeros((128, 1024 - VOCAB), f32)], axis=1)
    n.tg[at.z, at.c] = padded.T.astype(bf16)
    tg_z = RingGather(
        out, at, "z",
        lambda i, hf: n.tg.at[i, at.c, span(hf, 1024)],
        lambda k: n.tg.at[pl.ds(0, k), at.c],
        n.tgz_m,
    )
    step(1)
    red_g.forward()
    text_back(0)
    step(0)
    text_back(1)
    step(1)
    text_back(2)

    def weight_grad(c):
        left, right = n.tri[:, c].reshape(256, 256), n.dob[lax.div(c, 3)].reshape(256, DD)
        g = dot(left.astype(f32).T.astype(bf16), right)
        for core in range(2):
            for zz in range(4):
                lo = 128 * (2 * zz + core)
                for a in range(4):
                    n.gas[core, a, c, :, 128 * zz : 128 * zz + 128] = g[64 * a : 64 * a + 64, lo : lo + 128].astype(bf16)

    step(0)
    text_back(3)
    red_t = reduce("x", "t", rows_half(2))
    step(1)
    red_g.finish()
    g = red_g.total()
    for b in range(8):
        n.gts[b] = g[:, 128 * b : 128 * b + 128].astype(bf16)
    n.gtr[at.s] = n.gts[at.s]
    tg_z.forward()
    step(0)
    step(1)
    got_gt = seq_all(n.gts, n.gtr, n.gt_m)
    loop(0, 4, weight_grad)
    theirs = n.gas.at[1 - at.c]
    wait_gar = out.one(theirs, n.gar, n.gar_m, at.sibling())
    step(0)
    step(1)
    red_t.forward()
    term = held[0].gain_term + held[1].gain_term
    n.dgs[at.s] = jnp.concatenate([term[:, 128 * b : 128 * b + 128] for b in range(8)], axis=0)
    got_dgs = seq_same(n.dgs, n.dgs_m)
    got_lc.wait_recv()
    lane = lax.broadcasted_iota(jnp.int32, (16, 128), 1)
    for m in range(2):
        losses = jnp.zeros((16, 128), f32)
        for k in range(8):
            losses = jnp.where(lane == 1 + k, n.lr[k, m], losses)
        n.lx[at.x, m] = losses
    got_lx = x_same(n.lx, n.lx_m)
    tg_z.finish()
    share_t = n.tg.at[:, at.c]
    wait_t = out.one(share_t, share_t, n.tgc_m, at.sibling())
    step(0)

    def features(m):
        def quarter(a):
            block = dot(n.ib[m, a].reshape(128, DD), n.pj[at.s], NT)
            for s in range(8):
                rows = [block[32 * b + 4 * s : 32 * b + 4 * s + 4] for b in range(4)]
                rows = jnp.concatenate(rows, axis=0).astype(bf16)
                n.sf[s % 2, s // 2, pl.ds(pl.multiple_of(64 * m + 16 * a, 16), 16), :] = rows

        loop(0, 4, quarter)

    def hot_before(m):
        prev = jnp.where(at.s > 0, n.idr[1, :, 512 * m : 512 * m + 512] - at.t * 128, -1)
        entry = lax.broadcasted_iota(jnp.int32, (128, 512), 0)
        return jnp.where(prev == entry, 1.0, 0.0).astype(bf16)

    features(0)
    red_t.finish()
    for b in range(4):
        n.t2_s[b] = red_t.total(lambda ref: ref[b]).astype(bf16)
    red_t2 = reduce("y", "t2", rows_half(64))
    wait_gar.wait_recv()
    for a in range(4):
        n.ga_s[a] = (n.gas[at.c, a].astype(f32) + n.gar[a].astype(f32)).astype(bf16)
    red_ga = reduce("x", "ga", rows_half(2))
    before = hot_before(0)

    def first_half(b):
        cols = pl.ds(pl.multiple_of(256 * b, 256), 256)
        rows = n.ib[0, :, :, :, cols].reshape(512, 256)
        g = dot(n.nt[:, 0:512], rows)
        n.raw[0, :, cols] = g[0:128]
        n.raw[1, :, cols] = g[128:256]
        n.raw[2, :, cols] = dot(before, rows)

    loop(0, 4, first_half)
    red_t2.forward()
    step(1)
    features(1)
    wait_sf = out.one(n.sf.at[1 - at.c], n.sfr, n.sfr_m, at.sibling())

    def proj_grad(d):
        to = lax.rem(at.z + d, 4)
        cols = pl.ds(pl.multiple_of(to * 256, 256), 256)
        held_part = jnp.concatenate([n.raw[0, :, cols], n.raw[1, :, cols]], axis=0)
        g = held_part + dot(n.nt[:, 512:1024], n.ib[1, :, :, :, cols].reshape(512, 256))
        n.gps[2 * to] = g[:, 0:128].astype(bf16)
        n.gps[2 * to + 1] = g[:, 128:256].astype(bf16)
    def send_proj(d):
        proj_grad(d)
        to = lax.rem(at.z + d, 4)
        for core in range(2):
            src = n.gps.at[2 * to + core]
            out.go(src, n.gpr.at[at.s], n.gp_m.at[0], n.gp_m.at[1], {"z": to, "core": core})

    wait_sf.wait_recv()
    for b in range(4):
        n.f_s[b] = (n.sf[at.c, b].astype(f32) + n.sfr[b].astype(f32)).astype(bf16)
    red_f = direct("z", "f")
    red_t2.finish()
    loop(1, 4, send_proj)
    proj_grad(0)
    n.gpr[at.s] = n.gps[at.s]
    theirs = 2 * at.z + 1 - at.c
    out.go(n.gps.at[theirs], n.gpr.at[at.s], n.gp_m.at[0], n.gp_m.at[1], at.sibling())
    out.sent_later(n.gps.at[pl.ds(0, 7)], n.gp_m.at[0])
    got_gp = out.bytes_of(n.gpr.at[pl.ds(0, 7)], n.gp_m.at[1])
    red_f.finish()
    fb = red_t2.total() + red_f.total()
    gback = fb * gain
    inner = jnp.sum(gback * hat, axis=1, keepdims=True)
    n.rd[at.t] = jnp.broadcast_to(inner, (128, 128)).T[0:8, :]
    got_rd = plane_same(n.rd, n.rd_m)
    n.tgn[at.s] = jnp.broadcast_to(jnp.sum(fb * hat, axis=0, keepdims=True), (8, 256))
    got_tgn = seq_same(n.tgn, n.tgn_m)
    before = hot_before(1)

    def second_half(b):
        cols = pl.ds(pl.multiple_of(256 * b, 256), 256)
        look = (n.raw[2, :, cols] + dot(before, n.ib[1, :, :, :, cols].reshape(512, 256))) * embed_scale
        n.lks[2 * b] = look[:, 0:128].astype(bf16)
        n.lks[2 * b + 1] = look[:, 128:256].astype(bf16)

    loop(0, 4, second_half)
    got_lk = seq_all(n.lks, n.lkr, n.lk_m)
    n.lkr[at.s] = n.lks[at.s]
    red_ga.forward()
    got_dgs.wait_recv()
    n.dgt[at.t] = jnp.sum(n.dgs[...], axis=0)
    got_dgt = plane_same(n.dgt, n.dgt_m)

    wait_t.wait_recv()
    got_nd.wait_recv()

    def table_grad(a):
        part = pl.ds(pl.multiple_of(256 * a, 256), 256)
        left = jnp.concatenate([n.tg[g // 2, g % 2, part, :] for g in range(8)], axis=1)
        for b in range(2):
            right = n.ndst[:, b].reshape(1024, 256)
            n.o_gtt[part, 256 * b : 256 * b + 256] = dot(left, right).astype(bf16)

    loop(0, 4, table_grad)
    red_ga.finish()
    for b in range(4):
        n.gz_s[b] = red_ga.total(lambda ref: ref[:, :, 128 * b : 128 * b + 128]).astype(bf16)
    red_gz = direct("z", "gz")
    got_rd.wait_recv()
    dots = twice(row_to_col(jnp.sum(n.rd[...], axis=0)[0:1, :], 128))
    n.o_gh[...] = scale * (gback - hat * (dots / D))
    got_tgn.wait_recv()
    n.o_tgain[...] = jnp.sum(n.tgn[...], axis=0)[0:1, :]
    got_dgt.wait_recv()
    n.o_dg[...] = jnp.sum(n.dgt[...], axis=0)
    got_lx.wait_recv()
    lane = lax.broadcasted_iota(jnp.int32, (128, 128), 1)
    losses = jnp.concatenate([n.lx[a, m] for m in range(2) for a in range(4)], axis=0)
    n.o_loss[...] = jnp.where(lane == 0, n.tlc[...], losses).T[0:9, :]
    got_gt.wait_recv()
    got_lk.wait_recv()
    for k in range(8):
        g = n.gtr[k].astype(f32)
        if k < 7:
            g = g + n.lkr[k + 1].astype(f32)
        n.o_gtab[k] = g
    got_gp.wait_recv()
    n.o_gp[...] = n.gpr[...]
    red_gz.finish()
    ga = red_gz.total()
    n.o_gqkv[...] = ga[0:3]
    n.o_gout[...] = ga[3]
    out.finish()


def write_kernel(*refs):
    count = len(refs) // 2
    for src, dst in zip(refs[:count], refs[count:]):
        dst[...] = src[...].astype(f32)


def write_outputs(results):
    shapes = [r.shape for r in results]
    shapes[3] = (VOCAB, 512)
    blocks = {1: (32, 256), 3: (256, 512), 4: (2, 256, 128), 5: (2, 128, 128)}

    def spec(i):
        block = blocks.get(i, shapes[i])
        moves = i in blocks
        return pl.BlockSpec(block, lambda g: (g if moves else 0,) + (0,) * (len(block) - 1))

    return pl.pallas_call(
        write_kernel,
        out_shape=[jax.ShapeDtypeStruct(shape, f32) for shape in shapes],
        grid=(4,),
        in_specs=[spec(i) for i in range(9)],
        out_specs=[spec(i) for i in range(9)],
        name="write",
    )(*results)


def on_device(
    hidden, text_gain, text_table, proj, audio_table, depth_gain, attn_qkv, attn_out, text_ids, audio_ids
):
    vmem = pl.BlockSpec(memory_space=pltpu.VMEM)
    hbm = pl.BlockSpec(memory_space=pl.ANY)
    outs = [
        ((9, 128), f32), ((128, 256), f32), ((1, 256), f32), ((1024, 512), bf16), ((8, 256, 128), bf16),
        ((8, 128, 128), f32), ((8, 128), f32), ((3, 64, 128), f32), ((64, 128), f32),
    ]
    results = pl.pallas_call(
        kernel,
        out_shape=[jax.ShapeDtypeStruct(shape, dtype) for shape, dtype in outs],
        in_specs=[vmem, vmem, hbm, hbm, hbm, vmem, vmem, vmem, vmem, vmem],
        out_specs=[vmem] * len(outs),
        scratch_shapes=[scratch_shape(entry) for entry in SCRATCH],
        name="head",
        compiler_params=pltpu.CompilerParams(
            collective_id=1, has_side_effects=True, vmem_limit_bytes=VMEM_LIMIT
        ),
    )(
        hidden, text_gain, text_table, proj, audio_table, depth_gain,
        jnp.transpose(attn_qkv, (1, 2, 0)), attn_out, text_ids[None, :], audio_ids.T,
    )
    losses, gh, tgain, gtt, gp, gtab, dg, gqkv, gout = write_outputs(results)
    return losses.T, gh, tgain[0], gtt.T, gp, gtab, dg.reshape(DD), jnp.transpose(gqkv, (2, 0, 1)), gout


def solution(mesh):
    fine = Mesh(mesh.devices.reshape(4, 2, 4, 4), ("z", "core", "x", "y"))
    seq = ("z", "core")
    tp = ("x", "y")
    in_specs = (
        P(seq, tp), P(tp), P(tp, None), P(None, tp, None), P(None, tp, None),
        P(), P(None, None, tp), P(tp, None), P(seq), P(seq, None),
    )
    out_specs = (
        P(seq, None), P(seq, tp), P(tp), P(seq, tp), P(None, tp, seq),
        P(None, tp, seq), P(), P(seq, None, tp), P(tp, seq),
    )
    return jax.shard_map(
        on_device, mesh=fine, in_specs=in_specs, out_specs=out_specs, check_vma=False
    )
```

time: 892 us -> 145 us (0.16)
  waiting for transfers between devices: 649 us -> 0 us
  Pallas kernels: 0 us -> 144 us
  blocking collectives: 114 us -> 0 us
  matrix products: 69 us -> 0 us
  local copies, waits for them, and re-layouts: 23.2 us -> 0 us
  other arithmetic: 20.9 us -> 0 us
  between operations: 14.5 us -> 0.81 us
    psum x4 -> x0, waiting for transfers between devices: 403 us -> none  [the longest x1 107 us: on_device(): depth_input = lax.psum(input_term, 'tp')]
    reduce_scatter x3 -> x0, waiting for transfers between devices: 186 us -> none  [the longest x1 92 us: on_device(): lax.psum_scatter(jnp.einsum('fd,fv->dv', full_normed, text_grad, preferre...]
    pallas_call x0 -> x2, Pallas kernels: none -> 144 us  [the longest x1 139 us: on_device(): pl.pallas_call(kernel, out_shape=[jax.ShapeDtypeStruct(shape, dtype) for...]
    psum x4 -> x0, blocking collectives: 114 us -> none  [the longest x2 64.5 us: on_device(): lax.psum((text_sum, text_chosen, audio_sum, audio_chosen), 'tp')]
    dot_general x23 -> x0, matrix products: 69 us -> none  [the longest x1 7.95 us: on_device(): jnp.einsum('fd,fv->dv', full_normed, text_grad, preferred_element_type=jn...]
    all_gather x1 -> x0, waiting for transfers between devices: 31.6 us -> none  [on_device(): full_normed = lax.all_gather(normed, 'tp', axis=1, tiled=True)]
    unnamed x14 -> x0, waiting for transfers between devices: 28 us -> none
    unnamed x85 -> x0, local copies, waits for them, and re-layouts: 18.3 us -> none
  transfers between devices with their start and end apart: 11 -> 0, of which waited for: 9 -> 0; matrix products, arithmetic and copies ran while one was open for 9% -> 0% of each run, Pallas kernels for 0% -> 0%
where the time goes in v1:
time: 145 us; the launch traced here: 144 us
  Pallas kernels  144 us (99%)
    pallas_call x1, Pallas kernels, on_device(): pl.pallas_call(kernel, out_shape=[jax.ShapeDtypeStruct(shape, dtype) for...  139 us
    pallas_call x1, Pallas kernels, write_outputs(): pl.pallas_call(write_kernel, out_shape=[jax.ShapeDtypeStruct(shape, f32)...  4.25 us

profile of v1, /device:TPU:1, one launch (start us, length us, event | category | flops | bytes accessed | tf_op | source)
XLA Modules:
  0.0 144.4 jit_solution(3756854475602140062)
XLA Ops:
  0.6 139.4 %head.1 = (f32[9,128]{1,0:T(8,128)}, f32[128,256]{1,0:T(8,128)}, f32[1,256]{1,0:T(1,128)}, bf16[1024,512]{1,0:T(8,128)(2,1)}, bf16[8,256,128]{2,1,0:T(8,128)(2,1...) custom-call(bf16[128,256]{1,0:T(8,128)(2,1)} %refs_0_.1, ...), custom_call_target="tpu_custom_call" | custom-call | tf_op jit(solution)/shard_map/head/pallas_call | solution.py:1007
  140.0 4.3 %write.1 = (f32[9,128]{1,0:T(8,128)}, f32[128,256]{1,0:T(8,128)}, f32[1,256]{1,0:T(1,128)}, f32[1000,512]{1,0:T(8,128)}, f32[8,256,128]{2,1,0:T(8,128)}, /*index...) custom-call(f32[9,128]{1,0:T(8,128)} %get-tuple-element.27.refs_0_, ...), custom_call_target="tpu_custom_call" | custom-call | tf_op jit(solution)/shard_map/write/pallas_call | solution.py:988

commit v2 on v1

--- a/solution.py
+++ b/solution.py
@@ -284,12 +284,13 @@
     *chain_scratch(0), *chain_scratch(1),
     ("dob", (2, 2, 4, 32, DD), bf16), ("qkv", (2, 3, 128, 256), bf16),
     ("ex", (2, 4, 128, 128), f32), ("ob", (2, 4, 32, DD), bf16),
-    ("gr", (2, 128, 512), bf16), ("tri", (2, 4, 128, 256), bf16),
+    ("gr", (2, 512, 128), bf16), ("tri", (2, 4, 128, 256), bf16), ("trt", (4, 256, 256), bf16),
     ("tab", (4, 128, DD), bf16), ("tab_m", 4, None),
-    ("tl", (128, VOCAB), f32), ("ts", (16, 8, 128), f32), ("ts_m", 2, None), ("tgr", (128, VOCAB), bf16),
+    ("tl", (VOCAB, 128), f32), ("ty", (4, 8, 128), f32), ("ty_m", 2, None), ("tx", (4, 8, 128), f32), ("tx_m", 2, None),
+    ("tgr", (128, VOCAB), bf16), ("tlr", (1, 128), f32),
     *ring_reduce_scratch("g", (128, DD), (64, DD)),
     ("lc", (8, 2, 16, 128), f32), ("lr", (8, 2, 16, 128), f32), ("lc_m", 2, None),
-    ("lx", (4, 2, 16, 128), f32), ("lx_m", 2, None), ("tlc", (128, 128), f32),
+    ("lx", (4, 2, 16, 128), f32), ("lx_m", 2, None),
     ("nt", (256, 1024), bf16), ("tg", (4, 2, 1024, 128), bf16), ("tgz_m", 4, None), ("tgc_m", 2, None),
     *ring_reduce_scratch("t", (4, 128, 256), (2, 128, 256)),
     *ring_reduce_scratch("t2", (128, 256), (64, 256)),
@@ -301,10 +302,11 @@
     *direct_scratch("gz", (4, 64, 128)),
     ("sf", (2, 4, 128, 256), bf16), ("sfr", (4, 128, 256), bf16), ("sfr_m", 2, None),
     *direct_scratch("f", (128, 256)),
-    ("gps", (8, 256, 128), bf16), ("gpr", (8, 256, 128), bf16), ("gp_m", 2, None),
-    ("lks", (8, 128, 128), bf16), ("lkr", (8, 128, 128), bf16), ("lk_m", 2, None),
+    ("gas_all", (8, 384, 128), bf16), ("gar_all", (8, 384, 128), bf16), ("gall_m", 2, None),
+    ("rel", (2, 2, 192, 128), bf16), ("rel_m", 3, None),
     ("gts", (8, 128, 128), bf16), ("gtr", (8, 128, 128), bf16), ("gt_m", 2, None),
-    ("dgs", (8, 8, 128), f32), ("dgs_m", 2, None), ("dgt", (16, 8, 128), f32), ("dgt_m", 2, None),
+    ("dgs", (8, 8, 128), f32), ("dgs_m", 2, None), ("dgy", (4, 8, 128), f32), ("dgy_m", 2, None),
+    ("dgx", (4, 8, 128), f32), ("dgx_m", 2, None),
     ("rd", (16, 8, 128), f32), ("rd_m", 2, None), ("tgn", (8, 8, 256), f32), ("tgn_m", 2, None),
 ]
 
@@ -527,23 +529,20 @@
         got.wait_recv()
         rows = n.ob[m].reshape(128, DD)
         tab = n.tab[...].reshape(512, DD)
-        logits = capped(dot(rows, tab, NT))
-        hot = mine.hot
-        sums = jnp.sum(jnp.exp(logits - soft_cap), axis=1, keepdims=True)
-        chosen = jnp.sum(jnp.where(hot, logits, 0.0), axis=1, keepdims=True)
-        lane = lax.broadcasted_iota(jnp.int32, (128, 128), 1)
-        packed = jnp.where(lane == 0, sums, jnp.where(lane == 1, chosen, 0.0))
+        logits = capped(dot(tab, rows, NT))
+        hot = mine.hot == lax.broadcasted_iota(jnp.int32, (512, 128), 0)
+        sums = jnp.sum(jnp.exp(logits - soft_cap), axis=0, keepdims=True)
+        chosen = jnp.sum(jnp.where(hot, logits, 0.0), axis=0, keepdims=True)
         e = half_of(m, "e")
-        e[at.y] = packed.T[0:8, :]
+        e[at.y] = jnp.concatenate([sums, chosen, jnp.zeros((6, 128), f32)], axis=0)
         got = y_same(e, half_of(m, "e_m"))
         yield
         got.wait_recv()
         total = jnp.sum(e[...], axis=0)
         lse_row = soft_cap + jnp.log(total[0:1, :])
-        prob = jnp.exp(logits - row_to_col(lse_row, 128)[:, 0:1])
-        grad = ((prob - jnp.where(hot, 1.0, 0.0)) * cap_slope(logits)).astype(bf16)
-        n.gr[m] = grad
-        terms = dot(grad, tab)
+        grad = (jnp.exp(logits - lse_row) - jnp.where(hot, 1.0, 0.0)) * cap_slope(logits)
+        n.gr[m] = grad.astype(bf16)
+        terms = dot(grad.T.astype(bf16), tab)
         for b in range(4):
             getattr(n, f"v{m}_s")[b] = terms[32 * b : 32 * b + 32].astype(bf16)
         red_v = direct("y", f"v{m}")
@@ -640,7 +639,7 @@
 
     def text_piece(i):
         feats = jnp.concatenate([n.nb[i // 2, 2 * (i % 2) + b] for b in range(2)], axis=1)
-        part = dot(feats, n.tt[:, 512 * i : 512 * i + 512], NT)
+        part = dot(n.tt[:, 512 * i : 512 * i + 512], feats, NT)
         if i == 0:
             n.tl[...] = part
         else:
@@ -722,10 +721,10 @@
     norm_x.finish()
     loads[2].wait()
     text_piece(0)
+    step(0)
     text_piece(1)
-    step(0)
-    text_piece(2)
-    step(1)
+    step(1)
+
     def two_blocks(to):
         return n.nb.at[lax.div(to, 2), pl.ds(2 * lax.rem(to, 2), 2)]
 
@@ -733,58 +732,60 @@
     got_nd = out.spread(at.sp, 8, two_blocks, n.ndst.at[at.s], n.nd_m, n.ndst)
     for m in range(2):
         row = n.idr[0, :, pl.ds(pl.multiple_of(at.x * 128 + 512 * m, 128), 128)]
-        local = jnp.where(((row >> 7) & 3) == at.y, ((row >> 9) << 7) | (row & 127), -1)
-        column = row_to_col(local.astype(f32), 128)[:, 0:1]
-        held[m].hot = column == lax.broadcasted_iota(jnp.int32, (128, 512), 1).astype(f32)
+        held[m].hot = jnp.where(((row >> 7) & 3) == at.y, ((row >> 9) << 7) | (row & 127), -1)
     tab_x.finish()
+    text_piece(2)
+    step(0)
+    step(1)
     text_piece(3)
     step(0)
-    step(1)
     text_piece(4)
-    step(0)
+    step(1)
     text_piece(5)
-    step(1)
+    step(0)
     text_piece(6)
+    step(1)
     text_piece(7)
-    step(0)
-    step(1)
     tl = capped(n.tl[...])
     n.tl[...] = tl
-    tid = row_to_col(n.tid[...].astype(f32), 128)[:, 0:1]
-    text_hot = tid == lax.broadcasted_iota(jnp.int32, (128, VOCAB), 1).astype(f32) + (at.t * VOCAB).astype(f32)
-    tsum = jnp.sum(jnp.exp(tl - soft_cap), axis=1, keepdims=True)
-    tchosen = jnp.sum(jnp.where(text_hot, tl, 0.0), axis=1, keepdims=True)
-    lane = lax.broadcasted_iota(jnp.int32, (128, 128), 1)
-    packed = jnp.where(lane == 0, tsum, jnp.where(lane == 1, tchosen, 0.0))
-    n.ts[at.t] = packed.T[0:8, :]
-    got_ts = plane_same(n.ts, n.ts_m)
-    step(0)
+    text_hot = lax.broadcasted_iota(jnp.int32, (VOCAB, 128), 0) == n.tid[...] - at.t * VOCAB
+    tsum = jnp.sum(jnp.exp(tl - soft_cap), axis=0, keepdims=True)
+    tchosen = jnp.sum(jnp.where(text_hot, tl, 0.0), axis=0, keepdims=True)
+    n.ty[at.y] = jnp.concatenate([tsum, tchosen, jnp.zeros((6, 128), f32)], axis=0)
+    got_ty = y_same(n.ty, n.ty_m)
+    step(0)
+    grads = jnp.concatenate([n.gr[0], n.gr[1]], axis=1)
+
     def vocab_grad(b):
-        part = n.gr[:, :, pl.ds(pl.multiple_of(128 * b, 128), 128)].reshape(256, 128)
-        n.g_s[b] = dot(part.astype(f32).T.astype(bf16), n.ob[...].reshape(256, DD)).astype(bf16)
+        cols = pl.ds(pl.multiple_of(256 * b, 256), 256)
+        g = dot(grads, n.ob[:, :, :, cols].reshape(256, 256))
+        for a in range(4):
+            n.g_s[a, :, cols] = g[128 * a : 128 * a + 128].astype(bf16)
 
     loop(0, 4, vocab_grad)
     red_g = reduce("x", "g", rows_half(64))
     step(1)
+    got_ty.wait_recv()
+    n.tx[at.x] = jnp.sum(n.ty[...], axis=0)
+    got_tx = x_same(n.tx, n.tx_m)
     got_lc = seq_all(n.lc, n.lr, n.lc_m)
     n.lr[at.s] = n.lc[at.s]
-    got_ts.wait_recv()
-    ttotal = jnp.sum(n.ts[...], axis=0)
+    step(0)
+    got_tx.wait_recv()
+    ttotal = jnp.sum(n.tx[...], axis=0)
     tlse_row = soft_cap + jnp.log(ttotal[0:1, :])
-    n.tlc[...] = row_to_col(tlse_row - ttotal[1:2, :], 128)
+    n.tlr[...] = tlse_row - ttotal[1:2, :]
     tl = n.tl[...]
-    tgrad = jnp.exp(tl - row_to_col(tlse_row, 128)[:, 0:1]) - jnp.where(text_hot, 1.0, 0.0)
-    tgrad = tgrad * cap_slope(tl)
-    n.tgr[...] = tgrad.astype(bf16)
-    step(0)
-    padded = jnp.concatenate([tgrad, jnp.zeros((128, 1024 - VOCAB), f32)], axis=1)
-    n.tg[at.z, at.c] = padded.T.astype(bf16)
+    tgrad = (jnp.exp(tl - tlse_row) - jnp.where(text_hot, 1.0, 0.0)) * cap_slope(tl)
+    padded = jnp.concatenate([tgrad, jnp.zeros((1024 - VOCAB, 128), f32)], axis=0)
+    n.tg[at.z, at.c] = padded.astype(bf16)
     tg_z = RingGather(
         out, at, "z",
         lambda i, hf: n.tg.at[i, at.c, span(hf, 1024)],
         lambda k: n.tg.at[pl.ds(0, k), at.c],
         n.tgz_m,
     )
+    n.tgr[...] = padded.T[:, 0:VOCAB].astype(bf16)
     step(1)
     red_g.forward()
     text_back(0)
@@ -792,34 +793,40 @@
     text_back(1)
     step(1)
     text_back(2)
-
-    def weight_grad(c):
-        left, right = n.tri[:, c].reshape(256, 256), n.dob[lax.div(c, 3)].reshape(256, DD)
-        g = dot(left.astype(f32).T.astype(bf16), right)
-        for core in range(2):
-            for zz in range(4):
-                lo = 128 * (2 * zz + core)
-                for a in range(4):
-                    n.gas[core, a, c, :, 128 * zz : 128 * zz + 128] = g[64 * a : 64 * a + 64, lo : lo + 128].astype(bf16)
-
     step(0)
     text_back(3)
     red_t = reduce("x", "t", rows_half(2))
     step(1)
+
+    for c in range(4):
+        n.trt[c] = n.tri[:, c].reshape(256, 256).astype(f32).T.astype(bf16)
+
+    def weight_grad(zz):
+        cols = pl.ds(pl.multiple_of(256 * zz, 256), 256)
+        to = pl.ds(pl.multiple_of(128 * zz, 128), 128)
+        g = dot(n.trt[0:3].reshape(768, 256), n.dob[0, :, :, :, cols].reshape(256, 256))
+        last = dot(n.trt[3], n.dob[1, :, :, :, cols].reshape(256, 256))
+        for core in range(2):
+            for a in range(4):
+                for c in range(4):
+                    rows = last[64 * a : 64 * a + 64] if c == 3 else g[256 * c + 64 * a : 256 * c + 64 * a + 64]
+                    n.gas[core, a, c, :, to] = rows[:, 128 * core : 128 * core + 128].astype(bf16)
+
+    step(0)
+    tg_z.forward()
     red_g.finish()
     g = red_g.total()
     for b in range(8):
         n.gts[b] = g[:, 128 * b : 128 * b + 128].astype(bf16)
+    got_gt = seq_all(n.gts, n.gtr, n.gt_m)
     n.gtr[at.s] = n.gts[at.s]
-    tg_z.forward()
-    step(0)
-    step(1)
-    got_gt = seq_all(n.gts, n.gtr, n.gt_m)
-    loop(0, 4, weight_grad)
+    step(1)
+    loop(0, 2, weight_grad)
+    step(0)
+    loop(2, 4, weight_grad)
+    step(1)
     theirs = n.gas.at[1 - at.c]
     wait_gar = out.one(theirs, n.gar, n.gar_m, at.sibling())
-    step(0)
-    step(1)
     red_t.forward()
     term = held[0].gain_term + held[1].gain_term
     n.dgs[at.s] = jnp.concatenate([term[:, 128 * b : 128 * b + 128] for b in range(8)], axis=0)
@@ -838,14 +845,13 @@
     step(0)
 
     def features(m):
-        def quarter(a):
-            block = dot(n.ib[m, a].reshape(128, DD), n.pj[at.s], NT)
+        block = dot(n.ib[m].reshape(512, DD), n.pj[at.s], NT)
+        for a in range(4):
             for s in range(8):
-                rows = [block[32 * b + 4 * s : 32 * b + 4 * s + 4] for b in range(4)]
+                lo = 128 * a + 4 * s
+                rows = [block[lo + 32 * b : lo + 32 * b + 4] for b in range(4)]
                 rows = jnp.concatenate(rows, axis=0).astype(bf16)
-                n.sf[s % 2, s // 2, pl.ds(pl.multiple_of(64 * m + 16 * a, 16), 16), :] = rows
-
-        loop(0, 4, quarter)
+                n.sf[s % 2, s // 2, 64 * m + 16 * a : 64 * m + 16 * a + 16, :] = rows
 
     def hot_before(m):
         prev = jnp.where(at.s > 0, n.idr[1, :, 512 * m : 512 * m + 512] - at.t * 128, -1)
@@ -861,48 +867,66 @@
     for a in range(4):
         n.ga_s[a] = (n.gas[at.c, a].astype(f32) + n.gar[a].astype(f32)).astype(bf16)
     red_ga = reduce("x", "ga", rows_half(2))
-    before = hot_before(0)
+    left0 = jnp.concatenate([n.nt[:, 0:512], hot_before(0)], axis=0)
 
     def first_half(b):
         cols = pl.ds(pl.multiple_of(256 * b, 256), 256)
-        rows = n.ib[0, :, :, :, cols].reshape(512, 256)
-        g = dot(n.nt[:, 0:512], rows)
-        n.raw[0, :, cols] = g[0:128]
-        n.raw[1, :, cols] = g[128:256]
-        n.raw[2, :, cols] = dot(before, rows)
+        g = dot(left0, n.ib[0, :, :, :, cols].reshape(512, 256))
+        for i in range(3):
+            n.raw[i, :, cols] = g[128 * i : 128 * i + 128]
 
     loop(0, 4, first_half)
     red_t2.forward()
     step(1)
     features(1)
     wait_sf = out.one(n.sf.at[1 - at.c], n.sfr, n.sfr_m, at.sibling())
+
+    left1 = jnp.concatenate([n.nt[:, 512:1024], hot_before(1)], axis=0)
 
     def proj_grad(d):
         to = lax.rem(at.z + d, 4)
         cols = pl.ds(pl.multiple_of(to * 256, 256), 256)
-        held_part = jnp.concatenate([n.raw[0, :, cols], n.raw[1, :, cols]], axis=0)
-        g = held_part + dot(n.nt[:, 512:1024], n.ib[1, :, :, :, cols].reshape(512, 256))
-        n.gps[2 * to] = g[:, 0:128].astype(bf16)
-        n.gps[2 * to + 1] = g[:, 128:256].astype(bf16)
+        g = dot(left1, n.ib[1, :, :, :, cols].reshape(512, 256))
+        g = g + jnp.concatenate([n.raw[i, :, cols] for i in range(3)], axis=0)
+        g = jnp.concatenate([g[0:256], g[256:384] * embed_scale], axis=0)
+        n.gas_all[2 * to, 0:384, :] = g[:, 0:128].astype(bf16)
+        n.gas_all[2 * to + 1, 0:384, :] = g[:, 128:256].astype(bf16)
+
     def send_proj(d):
         proj_grad(d)
         to = lax.rem(at.z + d, 4)
         for core in range(2):
-            src = n.gps.at[2 * to + core]
-            out.go(src, n.gpr.at[at.s], n.gp_m.at[0], n.gp_m.at[1], {"z": to, "core": core})
-
+            src = n.gas_all.at[2 * to + core]
+            out.go(src, n.gar_all.at[at.s], n.gall_m.at[0], n.gall_m.at[1], {"z": to, "core": core})
+
+    right, far, left = lax.rem(at.z + 1, 4), lax.rem(at.z + 2, 4), lax.rem(at.z + 3, 4)
+    low, high = pl.ds(0, 192), pl.ds(192, 192)
+    proj_grad(2)
+    for core in range(2):
+        src = n.gas_all.at[2 * far + core]
+        out.go(src.at[low], n.rel.at[0, core], n.rel_m.at[0], n.rel_m.at[1], {"z": right})
+        out.go(src.at[high], n.rel.at[1, core], n.rel_m.at[0], n.rel_m.at[2], {"z": left})
     wait_sf.wait_recv()
     for b in range(4):
         n.f_s[b] = (n.sf[at.c, b].astype(f32) + n.sfr[b].astype(f32)).astype(bf16)
     red_f = direct("z", "f")
     red_t2.finish()
-    loop(1, 4, send_proj)
+    send_proj(1)
+    send_proj(3)
+    out.bytes_of(n.rel.at[0], n.rel_m.at[1]).wait_recv()
+    out.bytes_of(n.rel.at[1], n.rel_m.at[2]).wait_recv()
+    for core in range(2):
+        there = n.gar_all.at[2 * left + at.c, low]
+        out.go(n.rel.at[0, core], there, n.gall_m.at[0], n.gall_m.at[1], {"z": right, "core": core})
+        there = n.gar_all.at[2 * right + at.c, high]
+        out.go(n.rel.at[1, core], there, n.gall_m.at[0], n.gall_m.at[1], {"z": left, "core": core})
+    out.sent_later(n.rel, n.rel_m.at[0])
     proj_grad(0)
-    n.gpr[at.s] = n.gps[at.s]
+    n.gar_all[at.s] = n.gas_all[at.s]
     theirs = 2 * at.z + 1 - at.c
-    out.go(n.gps.at[theirs], n.gpr.at[at.s], n.gp_m.at[0], n.gp_m.at[1], at.sibling())
-    out.sent_later(n.gps.at[pl.ds(0, 7)], n.gp_m.at[0])
-    got_gp = out.bytes_of(n.gpr.at[pl.ds(0, 7)], n.gp_m.at[1])
+    out.go(n.gas_all.at[theirs], n.gar_all.at[at.s], n.gall_m.at[0], n.gall_m.at[1], at.sibling())
+    out.sent_later(n.gas_all.at[pl.ds(0, 7)], n.gall_m.at[0])
+    got_all = out.bytes_of(n.gar_all.at[pl.ds(0, 7)], n.gall_m.at[1])
     red_f.finish()
     fb = red_t2.total() + red_f.total()
     gback = fb * gain
@@ -911,33 +935,25 @@
     got_rd = plane_same(n.rd, n.rd_m)
     n.tgn[at.s] = jnp.broadcast_to(jnp.sum(fb * hat, axis=0, keepdims=True), (8, 256))
     got_tgn = seq_same(n.tgn, n.tgn_m)
-    before = hot_before(1)
-
-    def second_half(b):
-        cols = pl.ds(pl.multiple_of(256 * b, 256), 256)
-        look = (n.raw[2, :, cols] + dot(before, n.ib[1, :, :, :, cols].reshape(512, 256))) * embed_scale
-        n.lks[2 * b] = look[:, 0:128].astype(bf16)
-        n.lks[2 * b + 1] = look[:, 128:256].astype(bf16)
-
-    loop(0, 4, second_half)
-    got_lk = seq_all(n.lks, n.lkr, n.lk_m)
-    n.lkr[at.s] = n.lks[at.s]
     red_ga.forward()
     got_dgs.wait_recv()
-    n.dgt[at.t] = jnp.sum(n.dgs[...], axis=0)
-    got_dgt = plane_same(n.dgt, n.dgt_m)
+    n.dgy[at.y] = jnp.sum(n.dgs[...], axis=0)
+    got_dgy = y_same(n.dgy, n.dgy_m)
 
     wait_t.wait_recv()
     got_nd.wait_recv()
 
     def table_grad(a):
-        part = pl.ds(pl.multiple_of(256 * a, 256), 256)
+        part = pl.ds(pl.multiple_of(512 * a, 512), 512)
         left = jnp.concatenate([n.tg[g // 2, g % 2, part, :] for g in range(8)], axis=1)
         for b in range(2):
             right = n.ndst[:, b].reshape(1024, 256)
             n.o_gtt[part, 256 * b : 256 * b + 256] = dot(left, right).astype(bf16)
 
-    loop(0, 4, table_grad)
+    loop(0, 2, table_grad)
+    got_dgy.wait_recv()
+    n.dgx[at.x] = jnp.sum(n.dgy[...], axis=0)
+    got_dgx = x_same(n.dgx, n.dgx_m)
     red_ga.finish()
     for b in range(4):
         n.gz_s[b] = red_ga.total(lambda ref: ref[:, :, 128 * b : 128 * b + 128]).astype(bf16)
@@ -947,21 +963,19 @@
     n.o_gh[...] = scale * (gback - hat * (dots / D))
     got_tgn.wait_recv()
     n.o_tgain[...] = jnp.sum(n.tgn[...], axis=0)[0:1, :]
-    got_dgt.wait_recv()
-    n.o_dg[...] = jnp.sum(n.dgt[...], axis=0)
     got_lx.wait_recv()
-    lane = lax.broadcasted_iota(jnp.int32, (128, 128), 1)
-    losses = jnp.concatenate([n.lx[a, m] for m in range(2) for a in range(4)], axis=0)
-    n.o_loss[...] = jnp.where(lane == 0, n.tlc[...], losses).T[0:9, :]
+    losses = jnp.concatenate([n.lx[a, m] for m in range(2) for a in range(4)], axis=0).T
+    n.o_loss[...] = jnp.concatenate([n.tlr[...], losses[1:9]], axis=0)
+    got_dgx.wait_recv()
+    n.o_dg[...] = jnp.sum(n.dgx[...], axis=0)
     got_gt.wait_recv()
-    got_lk.wait_recv()
+    got_all.wait_recv()
+    n.o_gp[...] = n.gar_all[:, 0:256, :]
     for k in range(8):
         g = n.gtr[k].astype(f32)
         if k < 7:
-            g = g + n.lkr[k + 1].astype(f32)
+            g = g + n.gar_all[k + 1, 256:384, :].astype(f32)
         n.o_gtab[k] = g
-    got_gp.wait_recv()
-    n.o_gp[...] = n.gpr[...]
     red_gz.finish()
     ga = red_gz.total()
     n.o_gqkv[...] = ga[0:3]

time: 145 us -> 143 us (0.986)
  Pallas kernels: 144 us -> 141 us
    pallas_call x1, Pallas kernels: 139 us -> 137 us  [on_device(): pl.pallas_call(kernel, out_shape=[jax.ShapeDtypeStruct(shape, dtype) for...]
where the time goes in v2:
time: 143 us; the launch traced here: 142 us
  Pallas kernels  141 us (99%)
    pallas_call x1, Pallas kernels, on_device(): pl.pallas_call(kernel, out_shape=[jax.ShapeDtypeStruct(shape, dtype) for...  137 us
    pallas_call x1, Pallas kernels, write_outputs(): pl.pallas_call(write_kernel, out_shape=[jax.ShapeDtypeStruct(shape, f32)...  4.25 us

profile of v2, /device:TPU:1, one launch (start us, length us, event | category | flops | bytes accessed | tf_op | source)
XLA Modules:
  0.0 141.9 jit_solution(11119170612791198226)
XLA Ops:
  0.6 136.9 %head.1 = (f32[9,128]{1,0:T(8,128)}, f32[128,256]{1,0:T(8,128)}, f32[1,256]{1,0:T(1,128)}, bf16[1024,512]{1,0:T(8,128)(2,1)}, bf16[8,256,128]{2,1,0:T(8,128)(2,1...) custom-call(bf16[128,256]{1,0:T(8,128)(2,1)} %refs_0_.1, ...), custom_call_target="tpu_custom_call" | custom-call | tf_op jit(solution)/shard_map/head/pallas_call | solution.py:1021
  137.5 4.3 %write.1 = (f32[9,128]{1,0:T(8,128)}, f32[128,256]{1,0:T(8,128)}, f32[1,256]{1,0:T(1,128)}, f32[1000,512]{1,0:T(8,128)}, f32[8,256,128]{2,1,0:T(8,128)}, /*index...) custom-call(f32[9,128]{1,0:T(8,128)} %get-tuple-element.27.refs_0_, ...), custom_call_target="tpu_custom_call" | custom-call | tf_op jit(solution)/shard_map/write/pallas_call | solution.py:1002

commit v3 on v2

--- a/solution.py
+++ b/solution.py
@@ -47,29 +47,28 @@
         self.y = lax.axis_index("y")
         self.s = self.z * 2 + self.c
         self.t = self.x * 4 + self.y
-
-    def ring(self, axis):
-        me = {"x": self.x, "y": self.y, "z": self.z}[axis]
-        return me, lax.rem(me + 1, 4), lax.rem(me + 2, 4), lax.rem(me + 3, 4)
-
-    def xp(self, d):
-        to = lax.rem(self.x + d, 4)
-        return to, {"x": to}
-
-    def yp(self, d):
-        to = lax.rem(self.y + d, 4)
-        return to, {"y": to}
-
-    def sp(self, d):
-        to = lax.rem(self.s + d, 8)
-        return to, {"z": lax.div(to, 2), "core": lax.rem(to, 2)}
-
-    def tp(self, d):
-        to = lax.rem(self.t + d, 16)
-        return to, {"x": lax.div(to, 4), "y": lax.rem(to, 4)}
-
-    def sibling(self):
-        return {"core": 1 - self.c}
+        z, c, x, y = self.z, self.c, self.x, self.y
+        self.sibling = (z, 1 - c, x, y)
+        self.known = {}
+        for d in range(1, 4):
+            to = lax.rem(x + d, 4)
+            self.known["x", d] = (to, (z, c, to, y))
+            to = lax.rem(y + d, 4)
+            self.known["y", d] = (to, (z, c, x, to))
+            to = lax.rem(z + d, 4)
+            self.known["z", d] = (to, (to, c, x, y))
+        for d in range(1, 8):
+            to = lax.rem(self.s + d, 8)
+            self.known["s", d] = (to, (lax.div(to, 2), lax.rem(to, 2), x, y))
+        for d in range(1, 16):
+            to = lax.rem(self.t + d, 16)
+            self.known["t", d] = (to, (z, c, lax.div(to, 4), lax.rem(to, 4)))
+
+    def peer(self, axis, d):
+        return self.known[axis, d]
+
+    def index(self, axis):
+        return {"x": self.x, "y": self.y, "z": self.z, "s": self.s, "t": self.t}[axis]
 
 
 class Sends:
@@ -85,7 +84,7 @@
     def bytes_of(self, ref, sem):
         return pltpu.make_async_remote_copy(
             src_ref=ref, dst_ref=ref, send_sem=sem, recv_sem=sem,
-            device_id=self.at.sibling(), device_id_type=MESH,
+            device_id=self.at.sibling, device_id_type=MESH,
         )
 
     def sent_later(self, ref, sem):
@@ -96,9 +95,9 @@
         self.sent_later(src, sems.at[0])
         return self.bytes_of(dst, sems.at[1])
 
-    def spread(self, peer, n, src, dst, sems, slots, all_bytes=None):
+    def spread(self, axis, n, src, dst, sems, slots, all_bytes=None):
         for d in range(1, n):
-            to, device = peer(d)
+            to, device = self.at.peer(axis, d)
             self.go(src(to), dst, sems.at[0], sems.at[1], device)
         if all_bytes is None:
             all_bytes = slots.at[pl.ds(0, n - 1)]
@@ -113,9 +112,9 @@
 class RingGather:
     def __init__(self, out, at, axis, part, slots, sems):
         self.out, self.part, self.sems, self.slots = out, part, sems, slots
-        me, self.right, far, self.left = at.ring(axis)
-        self.to_right, self.to_left = {axis: self.right}, {axis: self.left}
-        block = part(me, None)
+        self.right, self.to_right = at.peer(axis, 1)
+        self.left, self.to_left = at.peer(axis, 3)
+        block = part(at.index(axis), None)
         out.go(block, block, sems.at[0], sems.at[1], self.to_right)
         out.go(block, block, sems.at[0], sems.at[2], self.to_left)
         out.sent_later(slots(3), sems.at[0])
@@ -136,9 +135,10 @@
 class RingReduce:
     def __init__(self, out, at, axis, blocks, half, bufs, sems):
         self.out, self.half, self.sems, self.blocks = out, half, sems, blocks
-        self.me, self.right, far, self.left = at.ring(axis)
+        self.me, far = at.index(axis), at.peer(axis, 2)[0]
+        self.right, self.to_right = at.peer(axis, 1)
+        self.left, self.to_left = at.peer(axis, 3)
         self.rl, self.rr, self.fa, self.fb = bufs
-        self.to_right, self.to_left = {axis: self.right}, {axis: self.left}
         s = blocks
         out.go(half(s.at[far], 0), self.fa, sems.at[0], sems.at[1], self.to_right)
         out.go(half(s.at[far], 1), self.fb, sems.at[0], sems.at[2], self.to_left)
@@ -168,10 +168,10 @@
 class DirectReduce:
     def __init__(self, out, at, axis, blocks, got, sems):
         self.blocks, self.got = blocks, got
-        self.me = at.ring(axis)[0]
+        self.me = at.index(axis)
         for d in (2, 1, 3):
-            to = lax.rem(self.me + d, 4)
-            out.go(blocks.at[to], got.at[d - 1], sems.at[0], sems.at[1], {axis: to})
+            to, device = at.peer(axis, d)
+            out.go(blocks.at[to], got.at[d - 1], sems.at[0], sems.at[1], device)
         out.sent_later(blocks.at[pl.ds(0, 3)], sems.at[0])
         self.wait = out.bytes_of(got, sems.at[1])
 
@@ -352,19 +352,19 @@
         )
 
     def seq_all(src, dst, sems):
-        return out.spread(at.sp, 8, lambda to: src.at[to], dst.at[at.s], sems, dst)
+        return out.spread("s", 8, lambda to: src.at[to], dst.at[at.s], sems, dst)
 
     def seq_same(ref, sems):
-        return out.spread(at.sp, 8, lambda to: ref.at[at.s], ref.at[at.s], sems, ref)
+        return out.spread("s", 8, lambda to: ref.at[at.s], ref.at[at.s], sems, ref)
 
     def plane_same(ref, sems):
-        return out.spread(at.tp, 16, lambda to: ref.at[at.t], ref.at[at.t], sems, ref)
+        return out.spread("t", 16, lambda to: ref.at[at.t], ref.at[at.t], sems, ref)
 
     def x_same(ref, sems):
-        return out.spread(at.xp, 4, lambda to: ref.at[at.x], ref.at[at.x], sems, ref)
+        return out.spread("x", 4, lambda to: ref.at[at.x], ref.at[at.x], sems, ref)
 
     def y_same(ref, sems):
-        return out.spread(at.yp, 4, lambda to: ref.at[at.y], ref.at[at.y], sems, ref)
+        return out.spread("y", 4, lambda to: ref.at[at.y], ref.at[at.y], sems, ref)
 
     loads = [
         pltpu.make_async_copy(src, dst, n.load.at[i])
@@ -376,10 +376,10 @@
         n.wb[at.x, c] = n.wqkv[c]
     n.wb[at.x, 3] = n.wout[...]
     barrier = pltpu.get_barrier_semaphore()
-    for d in range(1, 16):
-        pl.semaphore_signal(barrier, inc=1, device_id=at.tp(d)[1], device_id_type=MESH)
-    for d in range(1, 8):
-        pl.semaphore_signal(barrier, inc=1, device_id=at.sp(d)[1], device_id_type=MESH)
+    for axis, count in (("t", 16), ("s", 8)):
+        for d in range(1, count):
+            device = at.peer(axis, d)[1]
+            pl.semaphore_signal(barrier, inc=1, device_id=device, device_id_type=MESH)
     h = n.hid[...].astype(f32)
     gain = n.gain[...].astype(f32)[None, :]
     dgain = n.dgain[...].astype(f32)[None, :]
@@ -603,18 +603,18 @@
         def part(axis, where, sems):
             return RingGather(out, at, axis, where, lambda k: where(pl.ds(0, k), None), sems)
 
-        def spread(peer, mine_is, where, sems):
+        def spread(axis, mine_is, where, sems):
             src = where(mine_is)
-            return out.spread(peer, 4, lambda to: src, src, sems, None, where(pl.ds(0, 3)))
+            return out.spread(axis, 4, lambda to: src, src, sems, None, where(pl.ds(0, 3)))
 
         low, high = pl.ds(0, 16), pl.ds(16, 16)
         ib = n.ib.at[m]
         if m == 0:
-            one = [spread(at.xp, at.x, lambda i: ib.at[i, at.y], n.i0x_m)]
+            one = [spread("x", at.x, lambda i: ib.at[i, at.y], n.i0x_m)]
         else:
             one = [
-                spread(at.xp, at.x, lambda i: ib.at[i, at.y, low], n.iax_m),
-                spread(at.yp, at.y, lambda i: ib.at[at.x, i, high], n.iby_m),
+                spread("x", at.x, lambda i: ib.at[i, at.y, low], n.iax_m),
+                spread("y", at.y, lambda i: ib.at[at.x, i, high], n.iby_m),
             ]
         yield
         one[0].wait_recv()
@@ -677,11 +677,11 @@
     step(1)
     norm_z.finish()
     share = n.ns.at[:, at.c]
-    wait_n = out.one(share, share, n.nc_m, at.sibling())
+    wait_n = out.one(share, share, n.nc_m, at.sibling)
     weights_z.finish()
-    for other in (weights.right, lax.rem(at.x + 2, 4), weights.left):
+    for other in (weights.right, at.peer("x", 2)[0], weights.left):
         part = n.wb.at[other, :, mine]
-        out.go(part, part, n.wc_m.at[0], n.wc_m.at[1], at.sibling())
+        out.go(part, part, n.wc_m.at[0], n.wc_m.at[1], at.sibling)
     out.sent_later(n.wb.at[pl.ds(0, 3), :, mine], n.wc_m.at[0])
     wait_w = out.bytes_of(n.wb.at[pl.ds(0, 3), :, mine], n.wc_m.at[1])
     got_ids.wait_recv()
@@ -729,7 +729,7 @@
         return n.nb.at[lax.div(to, 2), pl.ds(2 * lax.rem(to, 2), 2)]
 
     n.ndst[at.s] = two_blocks(at.s)[...]
-    got_nd = out.spread(at.sp, 8, two_blocks, n.ndst.at[at.s], n.nd_m, n.ndst)
+    got_nd = out.spread("s", 8, two_blocks, n.ndst.at[at.s], n.nd_m, n.ndst)
     for m in range(2):
         row = n.idr[0, :, pl.ds(pl.multiple_of(at.x * 128 + 512 * m, 128), 128)]
         held[m].hot = jnp.where(((row >> 7) & 3) == at.y, ((row >> 9) << 7) | (row & 127), -1)
@@ -826,7 +826,7 @@
     loop(2, 4, weight_grad)
     step(1)
     theirs = n.gas.at[1 - at.c]
-    wait_gar = out.one(theirs, n.gar, n.gar_m, at.sibling())
+    wait_gar = out.one(theirs, n.gar, n.gar_m, at.sibling)
     red_t.forward()
     term = held[0].gain_term + held[1].gain_term
     n.dgs[at.s] = jnp.concatenate([term[:, 128 * b : 128 * b + 128] for b in range(8)], axis=0)
@@ -841,7 +841,7 @@
     got_lx = x_same(n.lx, n.lx_m)
     tg_z.finish()
     share_t = n.tg.at[:, at.c]
-    wait_t = out.one(share_t, share_t, n.tgc_m, at.sibling())
+    wait_t = out.one(share_t, share_t, n.tgc_m, at.sibling)
     step(0)
 
     def features(m):
@@ -879,7 +879,7 @@
     red_t2.forward()
     step(1)
     features(1)
-    wait_sf = out.one(n.sf.at[1 - at.c], n.sfr, n.sfr_m, at.sibling())
+    wait_sf = out.one(n.sf.at[1 - at.c], n.sfr, n.sfr_m, at.sibling)
 
     left1 = jnp.concatenate([n.nt[:, 512:1024], hot_before(1)], axis=0)
 
@@ -897,15 +897,15 @@
         to = lax.rem(at.z + d, 4)
         for core in range(2):
             src = n.gas_all.at[2 * to + core]
-            out.go(src, n.gar_all.at[at.s], n.gall_m.at[0], n.gall_m.at[1], {"z": to, "core": core})
-
-    right, far, left = lax.rem(at.z + 1, 4), lax.rem(at.z + 2, 4), lax.rem(at.z + 3, 4)
+            out.go(src, n.gar_all.at[at.s], n.gall_m.at[0], n.gall_m.at[1], (to, core, at.x, at.y))
+
+    (right, to_right), (far, _), (left, to_left) = [at.peer("z", d) for d in (1, 2, 3)]
     low, high = pl.ds(0, 192), pl.ds(192, 192)
     proj_grad(2)
     for core in range(2):
         src = n.gas_all.at[2 * far + core]
-        out.go(src.at[low], n.rel.at[0, core], n.rel_m.at[0], n.rel_m.at[1], {"z": right})
-        out.go(src.at[high], n.rel.at[1, core], n.rel_m.at[0], n.rel_m.at[2], {"z": left})
+        out.go(src.at[low], n.rel.at[0, core], n.rel_m.at[0], n.rel_m.at[1], to_right)
+        out.go(src.at[high], n.rel.at[1, core], n.rel_m.at[0], n.rel_m.at[2], to_left)
     wait_sf.wait_recv()
     for b in range(4):
         n.f_s[b] = (n.sf[at.c, b].astype(f32) + n.sfr[b].astype(f32)).astype(bf16)
@@ -917,14 +917,14 @@
     out.bytes_of(n.rel.at[1], n.rel_m.at[2]).wait_recv()
     for core in range(2):
         there = n.gar_all.at[2 * left + at.c, low]
-        out.go(n.rel.at[0, core], there, n.gall_m.at[0], n.gall_m.at[1], {"z": right, "core": core})
+        out.go(n.rel.at[0, core], there, n.gall_m.at[0], n.gall_m.at[1], (right, core, at.x, at.y))
         there = n.gar_all.at[2 * right + at.c, high]
-        out.go(n.rel.at[1, core], there, n.gall_m.at[0], n.gall_m.at[1], {"z": left, "core": core})
+        out.go(n.rel.at[1, core], there, n.gall_m.at[0], n.gall_m.at[1], (left, core, at.x, at.y))
     out.sent_later(n.rel, n.rel_m.at[0])
     proj_grad(0)
     n.gar_all[at.s] = n.gas_all[at.s]
     theirs = 2 * at.z + 1 - at.c
-    out.go(n.gas_all.at[theirs], n.gar_all.at[at.s], n.gall_m.at[0], n.gall_m.at[1], at.sibling())
+    out.go(n.gas_all.at[theirs], n.gar_all.at[at.s], n.gall_m.at[0], n.gall_m.at[1], at.sibling)
     out.sent_later(n.gas_all.at[pl.ds(0, 7)], n.gall_m.at[0])
     got_all = out.bytes_of(n.gar_all.at[pl.ds(0, 7)], n.gall_m.at[1])
     red_f.finish()
@@ -992,7 +992,7 @@
 def write_outputs(results):
     shapes = [r.shape for r in results]
     shapes[3] = (VOCAB, 512)
-    blocks = {1: (32, 256), 3: (256, 512), 4: (2, 256, 128), 5: (2, 128, 128)}
+    blocks = {1: (64, 256), 3: (512, 512), 4: (4, 256, 128), 5: (4, 128, 128)}
 
     def spec(i):
         block = blocks.get(i, shapes[i])
@@ -1002,7 +1002,7 @@
     return pl.pallas_call(
         write_kernel,
         out_shape=[jax.ShapeDtypeStruct(shape, f32) for shape in shapes],
-        grid=(4,),
+        grid=(2,),
         in_specs=[spec(i) for i in range(9)],
         out_specs=[spec(i) for i in range(9)],
         name="write",

time: 143 us -> 142 us (level)
  no operation moved by 1% of the time
where the time goes in v3:
time: 142 us
  Pallas kernels  141 us (99%)
    pallas_call x1, Pallas kernels, on_device(): pl.pallas_call(kernel, out_shape=[jax.ShapeDtypeStruct(shape, dtype) for...  138 us
    pallas_call x1, Pallas kernels, write_outputs(): pl.pallas_call(write_kernel, out_shape=[jax.ShapeDtypeStruct(shape, f32)...  3.36 us

profile of v3, /device:TPU:1, one launch (start us, length us, event | category | flops | bytes accessed | tf_op | source)
XLA Modules:
  0.0 141.7 jit_solution(14202506110882591138)
XLA Ops:
  0.6 137.6 %head.1 = (f32[9,128]{1,0:T(8,128)}, f32[128,256]{1,0:T(8,128)}, f32[1,256]{1,0:T(1,128)}, bf16[1024,512]{1,0:T(8,128)(2,1)}, bf16[8,256,128]{2,1,0:T(8,128)(2,1...) custom-call(bf16[128,256]{1,0:T(8,128)(2,1)} %refs_0_.1, ...), custom_call_target="tpu_custom_call" | custom-call | tf_op jit(solution)/shard_map/head/pallas_call | solution.py:1021
  138.2 3.4 %write.1 = (f32[9,128]{1,0:T(8,128)}, f32[128,256]{1,0:T(8,128)}, f32[1,256]{1,0:T(1,128)}, f32[1000,512]{1,0:T(8,128)}, f32[8,256,128]{2,1,0:T(8,128)}, /*index...) custom-call(f32[9,128]{1,0:T(8,128)} %get-tuple-element.27.refs_0_, ...), custom_call_target="tpu_custom_call" | custom-call | tf_op jit(solution)/shard_map/write/pallas_call | solution.py:1002

commit v4 on v3

--- a/solution.py
+++ b/solution.py
@@ -96,7 +96,8 @@
         return self.bytes_of(dst, sems.at[1])
 
     def spread(self, axis, n, src, dst, sems, slots, all_bytes=None):
-        for d in range(1, n):
+        order = {4: (2, 1, 3), 8: (4, 3, 5, 2, 6, 1, 7)}.get(n, range(1, n))
+        for d in order:
             to, device = self.at.peer(axis, d)
             self.go(src(to), dst, sems.at[0], sems.at[1], device)
         if all_bytes is None:
@@ -721,8 +722,9 @@
     norm_x.finish()
     loads[2].wait()
     text_piece(0)
-    step(0)
     text_piece(1)
+    step(0)
+    text_piece(2)
     step(1)
 
     def two_blocks(to):
@@ -733,18 +735,15 @@
     for m in range(2):
         row = n.idr[0, :, pl.ds(pl.multiple_of(at.x * 128 + 512 * m, 128), 128)]
         held[m].hot = jnp.where(((row >> 7) & 3) == at.y, ((row >> 9) << 7) | (row & 127), -1)
+    text_piece(3)
     tab_x.finish()
-    text_piece(2)
-    step(0)
-    step(1)
-    text_piece(3)
     step(0)
     text_piece(4)
     step(1)
     text_piece(5)
     step(0)
+    step(1)
     text_piece(6)
-    step(1)
     text_piece(7)
     tl = capped(n.tl[...])
     n.tl[...] = tl
@@ -754,6 +753,7 @@
     n.ty[at.y] = jnp.concatenate([tsum, tchosen, jnp.zeros((6, 128), f32)], axis=0)
     got_ty = y_same(n.ty, n.ty_m)
     step(0)
+    step(1)
     grads = jnp.concatenate([n.gr[0], n.gr[1]], axis=1)
 
     def vocab_grad(b):
@@ -764,13 +764,13 @@
 
     loop(0, 4, vocab_grad)
     red_g = reduce("x", "g", rows_half(64))
-    step(1)
     got_ty.wait_recv()
     n.tx[at.x] = jnp.sum(n.ty[...], axis=0)
     got_tx = x_same(n.tx, n.tx_m)
+    step(0)
+    step(1)
     got_lc = seq_all(n.lc, n.lr, n.lc_m)
     n.lr[at.s] = n.lc[at.s]
-    step(0)
     got_tx.wait_recv()
     ttotal = jnp.sum(n.tx[...], axis=0)
     tlse_row = soft_cap + jnp.log(ttotal[0:1, :])
@@ -786,16 +786,17 @@
         n.tgz_m,
     )
     n.tgr[...] = padded.T[:, 0:VOCAB].astype(bf16)
+    step(0)
+    text_back(0)
     step(1)
     red_g.forward()
-    text_back(0)
-    step(0)
     text_back(1)
-    step(1)
+    step(0)
     text_back(2)
-    step(0)
+    step(1)
     text_back(3)
     red_t = reduce("x", "t", rows_half(2))
+    step(0)
     step(1)
 
     for c in range(4):
@@ -902,14 +903,14 @@
     (right, to_right), (far, _), (left, to_left) = [at.peer("z", d) for d in (1, 2, 3)]
     low, high = pl.ds(0, 192), pl.ds(192, 192)
     proj_grad(2)
+    wait_sf.wait_recv()
+    for b in range(4):
+        n.f_s[b] = (n.sf[at.c, b].astype(f32) + n.sfr[b].astype(f32)).astype(bf16)
+    red_f = direct("z", "f")
     for core in range(2):
         src = n.gas_all.at[2 * far + core]
         out.go(src.at[low], n.rel.at[0, core], n.rel_m.at[0], n.rel_m.at[1], to_right)
         out.go(src.at[high], n.rel.at[1, core], n.rel_m.at[0], n.rel_m.at[2], to_left)
-    wait_sf.wait_recv()
-    for b in range(4):
-        n.f_s[b] = (n.sf[at.c, b].astype(f32) + n.sfr[b].astype(f32)).astype(bf16)
-    red_f = direct("z", "f")
     red_t2.finish()
     send_proj(1)
     send_proj(3)

time: 142 us -> 146 us (1.028)
  Pallas kernels: 141 us -> 145 us
    pallas_call x1, Pallas kernels: 138 us -> 142 us  [on_device(): pl.pallas_call(kernel, out_shape=[jax.ShapeDtypeStruct(shape, dtype) for...]
where the time goes in v4:
time: 146 us
  Pallas kernels  145 us (99%)
    pallas_call x1, Pallas kernels, on_device(): pl.pallas_call(kernel, out_shape=[jax.ShapeDtypeStruct(shape, dtype) for...  142 us
    pallas_call x1, Pallas kernels, write_outputs(): pl.pallas_call(write_kernel, out_shape=[jax.ShapeDtypeStruct(shape, f32)...  3.36 us

profile of v4, /device:TPU:1, one launch (start us, length us, event | category | flops | bytes accessed | tf_op | source)
XLA Modules:
  0.0 146.1 jit_solution(4252327937467313271)
XLA Ops:
  0.6 141.9 %head.1 = (f32[9,128]{1,0:T(8,128)}, f32[128,256]{1,0:T(8,128)}, f32[1,256]{1,0:T(1,128)}, bf16[1024,512]{1,0:T(8,128)(2,1)}, bf16[8,256,128]{2,1,0:T(8,128)(2,1...) custom-call(bf16[128,256]{1,0:T(8,128)(2,1)} %refs_0_.1, ...), custom_call_target="tpu_custom_call" | custom-call | tf_op jit(solution)/shard_map/head/pallas_call | solution.py:1022
  142.5 3.4 %write.1 = (f32[9,128]{1,0:T(8,128)}, f32[128,256]{1,0:T(8,128)}, f32[1,256]{1,0:T(1,128)}, f32[1000,512]{1,0:T(8,128)}, f32[8,256,128]{2,1,0:T(8,128)}, /*index...) custom-call(f32[9,128]{1,0:T(8,128)} %get-tuple-element.27.refs_0_, ...), custom_call_target="tpu_custom_call" | custom-call | tf_op jit(solution)/shard_map/write/pallas_call | solution.py:1003

commit v5 on v3

--- a/solution.py
+++ b/solution.py
@@ -368,7 +368,7 @@
 
     loads = [
         pltpu.make_async_copy(src, dst, n.load.at[i])
-        for i, (src, dst) in enumerate([(n.proj, n.pj), (n.audio, n.au), (n.table, n.tt)])
+        for i, (src, dst) in enumerate([(n.audio, n.au), (n.proj, n.pj), (n.table, n.tt)])
     ]
     for copy in loads:
         copy.start()
@@ -389,6 +389,16 @@
     )
     n.idb[at.s] = n.ids[...]
     unscaled = (h * gain).astype(bf16)
+    loads[0].wait()
+    entry = (lax.broadcasted_iota(jnp.int32, (128, 128), 1) + at.t * 128).astype(f32)
+    n.look[0] = jnp.zeros((128, DD), bf16)
+
+    def look_step(k):
+        column = row_to_col(n.ids[pl.ds(k, 1), :].astype(f32), 128)
+        hot = jnp.where(column == entry, 1.0, 0.0).astype(bf16)
+        n.look[k + 1] = (dot(hot, n.au[k]) * embed_scale).astype(bf16)
+
+    loop(0, 7, look_step)
     pl.semaphore_wait(barrier, 22)
 
     got_ssq = plane_same(n.ssq, n.ssq_m)
@@ -401,22 +411,12 @@
         n.wb_m,
     )
     got_ids = seq_same(n.idb, n.idb_m)
-    loads[0].wait()
+    loads[1].wait()
 
     def raw_step(k):
         n.raw[k] = dot(unscaled, n.pj[k])
 
     loop(0, 8, raw_step)
-    loads[1].wait()
-    entry = (lax.broadcasted_iota(jnp.int32, (128, 128), 1) + at.t * 128).astype(f32)
-    n.look[0] = jnp.zeros((128, DD), bf16)
-
-    def look_step(k):
-        column = row_to_col(n.ids[pl.ds(k, 1), :].astype(f32), 128)
-        hot = jnp.where(column == entry, 1.0, 0.0).astype(bf16)
-        n.look[k + 1] = (dot(hot, n.au[k]) * embed_scale).astype(bf16)
-
-    loop(0, 7, look_step)
     got_ssq.wait_recv()
     scale = row_to_col(lax.rsqrt(jnp.sum(n.ssq[...], axis=0)[0:1, :] / D + epsilon), 128)
     column = scale[:, 0:1]
@@ -754,6 +754,12 @@
     n.ty[at.y] = jnp.concatenate([tsum, tchosen, jnp.zeros((6, 128), f32)], axis=0)
     got_ty = y_same(n.ty, n.ty_m)
     step(0)
+    step(1)
+    got_ty.wait_recv()
+    n.tx[at.x] = jnp.sum(n.ty[...], axis=0)
+    got_tx = x_same(n.tx, n.tx_m)
+    got_lc = seq_all(n.lc, n.lr, n.lc_m)
+    n.lr[at.s] = n.lc[at.s]
     grads = jnp.concatenate([n.gr[0], n.gr[1]], axis=1)
 
     def vocab_grad(b):
@@ -764,12 +770,6 @@
 
     loop(0, 4, vocab_grad)
     red_g = reduce("x", "g", rows_half(64))
-    step(1)
-    got_ty.wait_recv()
-    n.tx[at.x] = jnp.sum(n.ty[...], axis=0)
-    got_tx = x_same(n.tx, n.tx_m)
-    got_lc = seq_all(n.lc, n.lr, n.lc_m)
-    n.lr[at.s] = n.lc[at.s]
     step(0)
     got_tx.wait_recv()
     ttotal = jnp.sum(n.tx[...], axis=0)
@@ -902,14 +902,14 @@
     (right, to_right), (far, _), (left, to_left) = [at.peer("z", d) for d in (1, 2, 3)]
     low, high = pl.ds(0, 192), pl.ds(192, 192)
     proj_grad(2)
+    wait_sf.wait_recv()
+    for b in range(4):
+        n.f_s[b] = (n.sf[at.c, b].astype(f32) + n.sfr[b].astype(f32)).astype(bf16)
+    red_f = direct("z", "f")
     for core in range(2):
         src = n.gas_all.at[2 * far + core]
         out.go(src.at[low], n.rel.at[0, core], n.rel_m.at[0], n.rel_m.at[1], to_right)
         out.go(src.at[high], n.rel.at[1, core], n.rel_m.at[0], n.rel_m.at[2], to_left)
-    wait_sf.wait_recv()
-    for b in range(4):
-        n.f_s[b] = (n.sf[at.c, b].astype(f32) + n.sfr[b].astype(f32)).astype(bf16)
-    red_f = direct("z", "f")
     red_t2.finish()
     send_proj(1)
     send_proj(3)

time: 142 us -> 144 us (1.014)
  Pallas kernels: 141 us -> 143 us
    pallas_call x1, Pallas kernels: 138 us -> 140 us  [on_device(): pl.pallas_call(kernel, out_shape=[jax.ShapeDtypeStruct(shape, dtype) for...]
where the time goes in v5:
time: 144 us
  Pallas kernels  143 us (99%)
    pallas_call x1, Pallas kernels, on_device(): pl.pallas_call(kernel, out_shape=[jax.ShapeDtypeStruct(shape, dtype) for...  140 us
    pallas_call x1, Pallas kernels, write_outputs(): pl.pallas_call(write_kernel, out_shape=[jax.ShapeDtypeStruct(shape, f32)...  3.36 us

profile of v5, /device:TPU:1, one launch (start us, length us, event | category | flops | bytes accessed | tf_op | source)
XLA Modules:
  0.0 143.8 jit_solution(7525961714902396723)
XLA Ops:
  0.6 139.7 %head.1 = (f32[9,128]{1,0:T(8,128)}, f32[128,256]{1,0:T(8,128)}, f32[1,256]{1,0:T(1,128)}, bf16[1024,512]{1,0:T(8,128)(2,1)}, bf16[8,256,128]{2,1,0:T(8,128)(2,1...) custom-call(bf16[128,256]{1,0:T(8,128)(2,1)} %refs_0_.1, ...), custom_call_target="tpu_custom_call" | custom-call | tf_op jit(solution)/shard_map/head/pallas_call | solution.py:1021
  140.3 3.4 %write.1 = (f32[9,128]{1,0:T(8,128)}, f32[128,256]{1,0:T(8,128)}, f32[1,256]{1,0:T(1,128)}, f32[1000,512]{1,0:T(8,128)}, f32[8,256,128]{2,1,0:T(8,128)}, /*index...) custom-call(f32[9,128]{1,0:T(8,128)} %get-tuple-element.27.refs_0_, ...), custom_call_target="tpu_custom_call" | custom-call | tf_op jit(solution)/shard_map/write/pallas_call | solution.py:1002
